TPU v7x, 256 devices: a whole 4x4x8 slice. The times are simulated.
256 devices in a mesh: lon: 64 (over z, x, core), lat: 4 (over y).
Axes of the slice: x: 4, y: 4, z: 8, core: 2. Of those that a mesh axis runs over, the one named last changes fastest.
Arguments:
- thermal_departure: float32 [90, 128, 8192], P(None, 'lat', 'lon'), may hold values from -6 to 6
- moisture_profile: float32 [90, 128, 8192], P(None, 'lat', 'lon'), may hold values from -6 to 6
- solar_elevation_factor: float32 [128, 8192], P('lat', 'lon'), may hold values from 0.1 to 1
- daylight_groups: int32 [128, 64], P('lat', 'lon'), may hold values from 0 to 1, as said below
- spreading_factor: float32 [128, 8192], P('lat', 'lon'), may hold values from 0.03 to 0.24
- entry_layer_matrix: float32 [512, 181], replicated, may hold values from -0.4375 to 0.4375
- entry_layer_offset: float32 [512], replicated, may hold values from -3 to 3
- inner_layer_matrices: float32 [2, 512, 512], replicated, may hold values from -0.25 to 0.25
- inner_layer_offsets: float32 [2, 512], replicated, may hold values from -3 to 3
- final_layer_matrix: float32 [90, 512], replicated, may hold values from -0.25 to 0.25
- final_layer_offset: float32 [90], replicated, may hold values from -3 to 3
Outputs:
- heating: float32 [90, 128, 8192], P(None, 'lat', 'lon')
- temp_next: float32 [90, 128, 8192], P(None, 'lat', 'lon')
Inputs may be any that keep to these rules, and one draw needn't show every extreme that they name: In every row the sunlit strips form one run of 32 consecutive strips, wrapping around, so daylight_groups[r, j] + daylight_groups[r, (j + 32) mod 64] == 1; row r and row r + 32 are complements of each other.
All inputs are finite; a program needn't handle non-finite values.
Results may differ from a plain program's by a relative error of at most 0.0001.
Values sent between devices are 32-bit elements; how exact they have to be, the bound alone decides.
No kernel may reach another device: no remote copies, remote signals or barrier semaphores. Data moves between devices by JAX's collectives and lax.ppermute only.
A program may use at most 64 MiB of HBM per device.

v0:
```python
import functools

import jax
import jax.numpy as jnp
from jax import lax
from jax.experimental import pallas as pl
from jax.experimental.pallas import tpu as pltpu
from jax.sharding import PartitionSpec as P

F32 = jnp.float32
BF16 = jnp.bfloat16
F8 = jnp.float8_e4m3fn

LEV = 90
PAD = 96
ROWS = 32
COLS = 128
HID = 512
FEAT = 181
KIN = 256
CHUNK = 8
GROUPS = 4
W_LO = 2.0**15
W_HI = 2.0**6
X_LO = 2.0**9

VMEM = pl.BlockSpec(memory_space=pltpu.VMEM)
SMEM = pl.BlockSpec(memory_space=pltpu.SMEM)


def split(x):
    hi = x.astype(BF16)
    return hi, (x - hi.astype(F32)).astype(BF16)


def lane_index():
    return lax.broadcasted_iota(jnp.int32, (PAD, COLS), 1)


def pack_kernel(t_ref, k_ref, up_ref, down_ref, west_ref, east_ref, row_s):
    row_s[...] = jnp.zeros_like(row_s)
    lane = lane_index()
    west = jnp.zeros((PAD, COLS), F32)
    east = jnp.zeros((PAD, COLS), F32)
    for r in range(ROWS):
        row_s[r, 0:LEV, :] = t_ref[:, r, :]
        row_s[r, LEV : LEV + 1, :] = k_ref[r : r + 1, :]
    for r in range(ROWS):
        block = row_s[r]
        place = 2 * (r + 1)
        here = (lane == place) | (lane == place + 1)
        west = jnp.where(here, pltpu.roll(block, place, 1), west)
        east = jnp.where(here, pltpu.roll(block, place + 2, 1), east)
    west_ref[...] = west
    east_ref[...] = east
    up_ref[0:PAD] = row_s[0]
    up_ref[PAD:] = row_s[1]
    down_ref[0:PAD] = row_s[ROWS - 1]
    down_ref[PAD:] = row_s[ROWS - 2]


def pack(t, k):
    edge = jax.ShapeDtypeStruct((2 * PAD, COLS), F32)
    side = jax.ShapeDtypeStruct((PAD, COLS), F32)
    return pl.pallas_call(
        pack_kernel,
        out_shape=(edge, edge, side, side),
        in_specs=[VMEM] * 2,
        out_specs=(VMEM,) * 4,
        scratch_shapes=[pltpu.VMEM((ROWS, PAD, COLS), F32)],
        compiler_params=pltpu.CompilerParams(vmem_limit_bytes=16 << 20),
        cost_estimate=pl.CostEstimate(flops=10**6, bytes_accessed=2 * 10**6, transcendentals=0),
    )(t, k)


def corner_kernel(north_ref, south_ref, west_ref, east_ref, w_out, e_out):
    lane = lane_index()
    west, east = west_ref[...], east_ref[...]
    for block, r in ((north_ref[0:PAD], -1), (south_ref[0:PAD], ROWS)):
        place = 2 * (r + 1)
        here = (lane == place) | (lane == place + 1)
        rolled = pltpu.roll(block, place, 1) if place else block
        west = jnp.where(here, rolled, west)
        east = jnp.where(here, pltpu.roll(block, place + 2, 1), east)
    w_out[...] = west
    e_out[...] = east


def corners(north, south, west, east):
    side = jax.ShapeDtypeStruct((PAD, COLS), F32)
    return pl.pallas_call(
        corner_kernel,
        out_shape=(side, side),
        in_specs=[VMEM] * 4,
        out_specs=(VMEM, VMEM),
        compiler_params=pltpu.CompilerParams(vmem_limit_bytes=8 << 20),
        cost_estimate=pl.CostEstimate(flops=10**5, bytes_accessed=4 * 10**5, transcendentals=0),
    )(north, south, west, east)


def lit_rows(lit_ref, list_s):
    for r in range(ROWS):
        list_s[r] = 0

    def step(r, carry):
        n, last = carry
        lit = lit_ref[r, 0] > 0

        @pl.when(lit)
        def _():
            list_s[n] = r

        return jnp.where(lit, n + 1, n), jnp.where(lit, r, last)

    n, last = lax.fori_loop(0, ROWS, step, (jnp.int32(0), jnp.int32(0)))

    def fill(i, _):
        list_s[i] = last
        return 0

    lax.fori_loop(n, ROWS, fill, 0)
    return n


def column_of(row, n):
    hi = row.astype(BF16)
    rest = row - hi.astype(F32)
    mid = rest.astype(BF16)
    low = (rest - mid.astype(F32)).astype(BF16)
    parts = jnp.concatenate([hi, mid, low, jnp.zeros((13, n), BF16)], axis=0)
    return lax.dot_general(
        parts, jnp.ones((16, COLS), BF16), (((0,), (0,)), ((), ())), preferred_element_type=F32
    )


def power_below(bound):
    scale = jnp.float32(1.0)
    for k in range(9):
        scale = jnp.where(bound > 440.0 * 2.0**k, scale * 0.5, scale)
    return scale


def put3(dst, w, n):
    hi, lo = split(w)
    dst[:, 0:n] = hi
    dst[:, n : 2 * n] = hi
    dst[:, 2 * n : 3 * n] = lo


def prepare(w1_ref, b1_ref, w2_ref, b2_ref, w4_ref, b4_ref, w1s, w2s, w28, w4s, bs, sc):
    w1 = w1_ref[...]
    put3(w1s, jnp.concatenate([w1 * 0.5, jnp.zeros((HID, KIN - FEAT), F32)], axis=1), KIN)
    for k in range(2):
        w = w2_ref[k] * 0.5
        hi = w.astype(BF16)
        w2s[k] = hi
        w28[k, :, 0:HID] = ((w - hi.astype(F32)) * W_LO).astype(F8)
        w28[k, :, HID : 2 * HID] = (w * W_HI).astype(F8)
    put3(w4s, jnp.concatenate([w4_ref[...], jnp.zeros((PAD - LEV, HID), F32)], axis=0), HID)
    bs[0:HID] = column_of(b1_ref[...] * 0.5, HID)
    for k in range(2):
        bs[(k + 1) * HID : (k + 2) * HID] = column_of(b2_ref[k : k + 1] * 0.5, HID)
    bs[3 * HID : 3 * HID + PAD] = jnp.concatenate(
        [column_of(b4_ref[...], LEV), jnp.zeros((PAD - LEV, COLS), F32)], axis=0
    )
    bound = 6.0 * jnp.max(jnp.sum(jnp.abs(w1), axis=1, keepdims=True)) + jnp.max(jnp.abs(b1_ref[...]))
    sc[0] = power_below(bound)
    bound = bound * jnp.max(jnp.sum(jnp.abs(w2_ref[0]), axis=1, keepdims=True)) + jnp.max(
        jnp.abs(b2_ref[...])
    )
    sc[1] = power_below(bound)


def half_silu(u):
    return u + u * jnp.tanh(u)


def dot3(w, x):
    hi, lo = split(x)
    return jnp.dot(w[...], jnp.concatenate([hi, lo, hi], axis=0), preferred_element_type=F32)


def parts8(x, scale):
    hi = x.astype(BF16)
    low = x - hi.astype(F32)
    eight = jnp.concatenate([(x * scale).astype(F8), (low * (scale * X_LO)).astype(F8)], axis=0)
    return hi, eight


def network_chunk(c, list_s, t_ref, m_ref, s_ref, w1s, w2s, w28, w4s, bs, sc, xs, put):
    rows = [list_s[c * CHUNK + j] for j in range(CHUNK)]
    n = CHUNK // GROUPS
    tile = lambda b: jnp.concatenate([b] * n, axis=1)
    scale = [sc[0], sc[1]]
    back = [1.0 / (W_LO * s) for s in scale]
    for j in range(CHUNK):
        cols = slice(j * COLS, (j + 1) * COLS)
        xs[0:LEV, cols] = t_ref[:, rows[j], :]
        xs[LEV : 2 * LEV, cols] = m_ref[:, rows[j], :]
        xs[2 * LEV : FEAT, cols] = s_ref[pl.ds(rows[j], 1), :]
    held = [None] * GROUPS
    for g in range(GROUPS):
        x = xs[:, g * n * COLS : (g + 1) * n * COLS]
        held[g] = parts8(half_silu(dot3(w1s, x) + tile(bs[0:HID])), scale[0])
    for k in range(2):
        for g in range(GROUPS):
            hi, eight = held[g]
            v = jnp.dot(w2s[k], hi, preferred_element_type=F32)
            v = v + jnp.dot(w28[k], eight, preferred_element_type=F32) * back[k]
            h = half_silu(v + tile(bs[(k + 1) * HID : (k + 2) * HID]))
            held[g] = parts8(h, scale[1]) if k == 0 else h
    for g in range(GROUPS):
        o = dot3(w4s, held[g]) + tile(bs[3 * HID : 3 * HID + PAD])
        for j in range(n):
            row = rows[g * n + j]
            put(g * n + j, row, o[:, j * COLS : (j + 1) * COLS] * s_ref[pl.ds(row, 1), :])


WEIGHTS = (
    ((HID, 3 * KIN), BF16),
    ((2, HID, HID), BF16),
    ((2, HID, 2 * HID), F8),
    ((PAD, 3 * HID), BF16),
    ((3 * HID + PAD, COLS), F32),
)
ROW_BLOCK = (CHUNK, PAD, COLS)


def first_kernel(lit, t, m, s, w1, b1, w2, b2, w4, b4, w1s, w2s, w28, w4s, bs, sc, out, list_s, xs):
    n = lit_rows(lit, list_s)

    @pl.when(n > 0)
    def _():
        prepare(w1, b1, w2, b2, w4, b4, w1s, w2s, w28, w4s, bs, sc)
        xs[176:KIN] = jnp.zeros((KIN - 176, CHUNK * COLS), F32)

        def put(j, row, value):
            out[j] = value

        network_chunk(0, list_s, t, m, s, w1s, w2s, w28, w4s, bs, sc, xs, put)


def first(lit, t, m, s, *weights):
    return pl.pallas_call(
        first_kernel,
        out_shape=tuple(jax.ShapeDtypeStruct(*w) for w in WEIGHTS)
        + (jax.ShapeDtypeStruct((2,), F32), jax.ShapeDtypeStruct(ROW_BLOCK, F32)),
        in_specs=[SMEM] + [VMEM] * 9,
        out_specs=(VMEM,) * 5 + (SMEM, VMEM),
        scratch_shapes=[pltpu.SMEM((ROWS,), jnp.int32), pltpu.VMEM((KIN, CHUNK * COLS), F32)],
        compiler_params=pltpu.CompilerParams(vmem_limit_bytes=32 << 20),
        cost_estimate=pl.CostEstimate(flops=5 * 10**9, bytes_accessed=8 * 10**6, transcendentals=0),
    )(lit, t, m, s, *weights)


def second_kernel(lit, t, m, s, w1s, w2s, w28, w4s, bs, sc, out, list_s, xs):
    n = lit_rows(lit, list_s)

    @pl.when(n > CHUNK)
    def _():
        xs[176:KIN] = jnp.zeros((KIN - 176, CHUNK * COLS), F32)

        def put(j, row, value):
            out[j] = value

        network_chunk(1, list_s, t, m, s, w1s, w2s, w28, w4s, bs, sc, xs, put)


def second(lit, t, m, s, *prepared):
    return pl.pallas_call(
        second_kernel,
        out_shape=jax.ShapeDtypeStruct(ROW_BLOCK, F32),
        in_specs=[SMEM] + [VMEM] * 8 + [SMEM],
        out_specs=VMEM,
        scratch_shapes=[pltpu.SMEM((ROWS,), jnp.int32), pltpu.VMEM((KIN, CHUNK * COLS), F32)],
        compiler_params=pltpu.CompilerParams(vmem_limit_bytes=32 << 20),
        cost_estimate=pl.CostEstimate(flops=5 * 10**9, bytes_accessed=8 * 10**6, transcendentals=0),
    )(lit, t, m, s, *prepared)


def last_kernel(
    lit, t, m, s, w1s, w2s, w28, w4s, bs, sc, heat_a, heat_b, k, north, south, mine_w, mine_e, west, east,
    heat_out, temp_out, list_s, xs, heat_s, state, step_s,
):
    n = lit_rows(lit, list_s)
    heat_s[...] = jnp.zeros_like(heat_s)

    for part, block in ((0, heat_a), (1, heat_b)):
        @pl.when(n > part * CHUNK)
        def _():
            for j in range(CHUNK):
                heat_s[list_s[part * CHUNK + j]] = block[j]

    @pl.when(n > 2 * CHUNK)
    def _():
        xs[176:KIN] = jnp.zeros((KIN - 176, CHUNK * COLS), F32)

        def put(j, row, value):
            heat_s[row] = value

        def one(c, _):
            network_chunk(c, list_s, t, m, s, w1s, w2s, w28, w4s, bs, sc, xs, put)
            return 0

        lax.fori_loop(2, (n + CHUNK - 1) // CHUNK, one, 0)

    state[0] = north[PAD:]
    state[1] = north[0:PAD]
    for r in range(ROWS):
        state[r + 2, 0:LEV, :] = t[:, r, :]
        state[r + 2, LEV : LEV + 1, :] = k[r : r + 1, :]
        state[r + 2, LEV + 1 : PAD, :] = jnp.zeros((PAD - LEV - 1, COLS), F32)
    state[ROWS + 2] = south[0:PAD]
    state[ROWS + 3] = south[PAD:]
    lane = lane_index()
    odd = lane % 2 == 1
    side = jnp.where(odd, west[...], east[...])

    def compact(far, own, towards):
        near = far[...]
        number = near[LEV : LEV + 1, :]
        around = (
            pltpu.roll(near, 2, 1)
            + pltpu.roll(near, COLS - 2, 1)
            + pltpu.roll(near, towards, 1)
            + pltpu.roll(own[...], towards, 1)
        )
        return near + number * (around - 4.0 * near)

    side_next = jnp.where(odd, compact(west, mine_w, 1), compact(east, mine_e, COLS - 1))
    first_lane, last_lane = lane == 0, lane == COLS - 1

    def substep(above, here, below, number, sides, r):
        edge = pltpu.roll(sides, (-(2 * r + 3)) % COLS, 1)
        left = jnp.where(first_lane, edge, pltpu.roll(here, 1, 1))
        right = jnp.where(last_lane, edge, pltpu.roll(here, COLS - 1, 1))
        return here + number * (above + below + left + right - 4.0 * here)

    for r in range(-1, ROWS + 1):
        number = state[r + 2, LEV : LEV + 1, :]
        step_s[r + 1] = substep(state[r + 1], state[r + 2], state[r + 3], number, side, r)
    for r in range(ROWS):
        number = state[r + 2, LEV : LEV + 1, :]
        done = substep(step_s[r], step_s[r + 1], step_s[r + 2], number, side_next, r)
        heat = heat_s[r]
        heat_out[:, r, :] = heat[0:LEV]
        temp_out[:, r, :] = (done + heat)[0:LEV]


def last(lit, t, m, s, prepared, *rest):
    whole = jax.ShapeDtypeStruct((LEV, ROWS, COLS), F32)
    return pl.pallas_call(
        last_kernel,
        out_shape=(whole, whole),
        in_specs=[SMEM] + [VMEM] * 8 + [SMEM] + [VMEM] * 9,
        out_specs=(VMEM, VMEM),
        scratch_shapes=[
            pltpu.SMEM((ROWS,), jnp.int32),
            pltpu.VMEM((KIN, CHUNK * COLS), F32),
            pltpu.VMEM((ROWS, PAD, COLS), F32),
            pltpu.VMEM((ROWS + 4, PAD, COLS), F32),
            pltpu.VMEM((ROWS + 2, PAD, COLS), F32),
        ],
        compiler_params=pltpu.CompilerParams(vmem_limit_bytes=40 << 20),
        cost_estimate=pl.CostEstimate(flops=10**10, bytes_accessed=8 * 10**6, transcendentals=0),
    )(lit, t, m, s, *prepared, *rest)


def on_device(t, m, s, lit, k, w1, b1, w2, b2, w4, b4):
    lats, lons = lax.axis_size("lat"), lax.axis_size("lon")
    up, down, west, east = pack(t, k)
    north = lax.ppermute(down, "lat", [(i, i + 1) for i in range(lats - 1)])
    south = lax.ppermute(up, "lat", [(i + 1, i) for i in range(lats - 1)])
    *prepared, heat_a = first(lit, t, m, s, w1, b1.reshape(1, HID), w2, b2, w4, b4.reshape(1, LEV))
    west, east = corners(north, south, west, east)
    from_east = lax.ppermute(west, "lon", [(i, (i - 1) % lons) for i in range(lons)])
    from_west = lax.ppermute(east, "lon", [(i, (i + 1) % lons) for i in range(lons)])
    heat_b = second(lit, t, m, s, *prepared)
    return last(lit, t, m, s, prepared, heat_a, heat_b, k, north, south, west, east, from_west, from_east)


def solution(mesh):
    whole, plane = P(None, "lat", "lon"), P("lat", "lon")
    return jax.shard_map(
        on_device,
        mesh=mesh,
        in_specs=(whole, whole, plane, plane, plane) + (P(),) * 6,
        out_specs=(whole, whole),
        check_vma=False,
    )
```

profile of v0, /device:TPU:16, one launch (start us, length us, event | category | flops | bytes accessed | tf_op | source)
XLA Modules:
  0.0 54.7 jit_solution(2728170147754951345)
XLA Ops:
  0.6 0.0 copy-start
  0.6 1.4 %copy-done = f32[90,32,128]{2,1,0:T(8,128)S(1)} copy-done((f32[90,32,128]{2,1,0:T(8,128)S(1)}, f32[90,32,128]{2,1,0:T(8,128)}, u32[]{:S(2)}) %copy-start) | copy-done | bytes 1474584
  2.0 0.0 copy-start.2
  2.0 0.7 %copy-done.2 = f32[32,128]{1,0:T(8,128)S(1)} copy-done((f32[32,128]{1,0:T(8,128)S(1)}, f32[32,128]{1,0:T(8,128)}, u32[]{:S(2)}) %copy-start.2) | copy-done | bytes 16408
  2.7 0.0 copy-start.1
  2.7 0.0 copy-start.7
  2.7 0.0 copy-start.8
  2.7 0.0 copy-start.9
  2.7 0.0 copy-start.10
  2.7 0.0 copy-start.11
  2.8 1.6 %shard_map.124 = (f32[192,128]{1,0:T(8,128)S(1)}, f32[192,128]{1,0:T(8,128)S(1)}, f32[96,128]{1,0:T(8,128)S(1)}, f32[96,128]{1,0:T(8,128)S(1)}) custom-call(f32[90,32,128]{2,1,0:T(8,128)S(1)} %copy-done, f32[32,128]{1,0:T(8,128)S(1)} %copy-done.2), custom_call_target="tpu_custom_call" | custom-call | flops 1000000 | bytes 2000000 | tf_op jit(solution)/shard_map/pallas_call | solution.py:65
  4.3 3.2 %collective-permute-start = (f32[192,128]{1,0:T(8,128)S(1)}, f32[192,128]{1,0:T(8,128)S(1)}, u32[]{:S(2)}, u32[]{:S(2)}) collective-permute-start(f32[192,128]{1,0:T(8,128)S(1)} %get-tuple-element.22), channel_id=1, source_target_pairs={{0,1},{1,2},{2,3},{4,5},{5,6},{6,7},{8,9},{9,10},{10,11},{12,13},{... | collective-permute-start | bytes 294920 | tf_op jit(solution)/shard_map/ppermute | solution.py:372
  7.5 2.7 %collective-permute-start.1 = (f32[192,128]{1,0:T(8,128)S(1)}, f32[192,128]{1,0:T(8,128)S(1)}, u32[]{:S(2)}, u32[]{:S(2)}) collective-permute-start(f32[192,128]{1,0:T(8,128)S(1)} %get-tuple-element.23), channel_id=1, source_target_pairs={{1,0},{2,1},{3,2},{5,4},{6,5},{7,6},{9,8},{10,9},{11,10},{13,12},{... | collective-permute-start | bytes 294920 | tf_op jit(solution)/shard_map/ppermute | solution.py:373
  10.2 0.7 %copy.16.lit = s32[32,1]{1,0:T(8,128)S(1)} copy(s32[32,1]{0,1:T(1,128)} %param.14) | data formatting | bytes 256 | tf_op args[3]
  10.9 1.2 %copy.14.w1 = f32[512,181]{1,0:T(8,128)S(1)} copy(f32[512,181]{0,1:T(8,128)} %param.16) | data formatting | bytes 741376 | tf_op args[5]
  12.1 0.0 copy-done.1
  12.1 0.0 copy-done.7
  12.2 0.0 copy-done.8
  12.2 0.0 copy-done.9
  12.2 0.0 copy-done.10
  12.2 0.0 copy-done.11
  12.2 0.0 copy-start.4
  12.2 1.6 %copy-done.4 = f32[2,512,512]{2,1,0:T(8,128)S(1)} copy-done((f32[2,512,512]{2,1,0:T(8,128)S(1)}, f32[2,512,512]{2,1,0:T(8,128)}, u32[]{:S(2)}) %copy-start.4) | copy-done | bytes 2097176
  13.8 0.0 copy-start.5
  13.8 1.4 %copy-done.5 = f32[90,32,128]{2,1,0:T(8,128)S(1)} copy-done((f32[90,32,128]{2,1,0:T(8,128)S(1)}, f32[90,32,128]{2,1,0:T(8,128)}, u32[]{:S(2)}) %copy-start.5) | copy-done | bytes 1474584
  15.2 7.2 %shard_map.122 = (bf16[512,768]{1,0:T(8,128)(2,1)S(1)}, bf16[2,512,512]{2,1,0:T(8,128)(2,1)S(1)}, f8e4m3fn[2,512,1024]{2,1,0:T(32,128)(4,1)S(1)}, bf16[96,1536]{...) custom-call(s32[32,1]{1,0:T(8,128)S(1)} %copy.16.lit, ...), custom_call_target="tpu_custom_call" | custom-call | flops 5000000000 | bytes 8000000 | tf_op jit(solution)/shard_map/pallas_call | solution.py:244
  22.4 0.0 collective-permute-done.north_ref.north
  22.4 0.0 collective-permute-done.1.south_ref.south
  22.4 0.1 shard_map.125
  22.5 7.0 %collective-permute-start.3 = (f32[96,128]{1,0:T(8,128)S(1)}, f32[96,128]{1,0:T(8,128)S(1)}, u32[]{:S(2)}, u32[]{:S(2)}) collective-permute-start(f32[96,128]{1,0:T(8,128)S(1)} %get-tuple-element.26.mine_w), channel_id=1, source_target_pairs={{0,252},{4,0},{8,4},{12,8},{16,12},{20,16},{24,20},{28,24},{32,28}... | collective-permute-start | bytes 147464 | tf_op jit(solution)/shard_map/ppermute | solution.py:376
  29.6 0.0 collective-permute-start.2
  29.6 0.0 copy-start.3
  29.6 0.0 copy-start.6
  29.6 6.0 %shard_map.123.heat_b = f32[8,96,128]{2,1,0:T(8,128)S(1)} custom-call(s32[32,1]{1,0:T(8,128)S(1)} %copy.16.lit, f32[90,32,128]{2,1,0:T(8,128)S(1)} %copy-done.1, f32[90,32,128]{2,1,0:T(8,128)S(1)} %copy-done.5, f32[32,128]{1,0:T(8,128)S(1)} %copy-done.8, bf16[512,768]{1,0:T(8,128)(2,1)S(1)} %get-tuple-element.15.w1s, ...), custom_call_target="tpu_custom_call" | custom-call | flops 5000000000 | bytes 8000000 | tf_op jit(solution)/shard_map/pallas_call | solution.py:270
  35.6 0.0 collective-permute-done.3.east
  35.6 0.8 %collective-permute-done.2.west = f32[96,128]{1,0:T(8,128)S(1)} collective-permute-done((f32[96,128]{1,0:T(8,128)S(1)}, f32[96,128]{1,0:T(8,128)S(1)}, u32[]{:S(2)}, u32[]{:S(2)}) %collective-permute-start.2) | collective-permute-done | bytes 49184 | tf_op jit(solution)/shard_map/ppermute | solution.py:377
  36.4 0.0 copy-done.3
  36.4 0.0 copy-done.6
  36.4 18.3 %shard_map.126 = (f32[90,32,128]{2,1,0:T(8,128)}, f32[90,32,128]{2,1,0:T(8,128)}) custom-call(s32[32,1]{1,0:T(8,128)S(1)} %copy.16.lit, f32[90,32,128]{2,1,0:T(8,128)S(1)} %copy-done.1, f32[90,32,128]{2,1,0:T(8,128)S(1)} %copy-done.6, f32[32,128]{1,0:T(8,128)S(1)} %copy-done.8, bf16[512,768]{1,0:T(8,128)(2,1)S(1)} %get-tuple-element.15.w1s, ...), custom_call_target="tpu_custom_call" | custom-call | flops 10000000000 | bytes 8000000 | tf_op jit(solution)/shard_map/pallas_call | solution.py:352
Async XLA Ops:
  0.6 1.4 %copy-start = (f32[90,32,128]{2,1,0:T(8,128)S(1)}, f32[90,32,128]{2,1,0:T(8,128)}, u32[]{:S(2)}) copy-start(f32[90,32,128]{2,1,0:T(8,128)} %t.5) | copy-start | bytes 4423684
  2.0 0.7 %copy-start.2 = (f32[32,128]{1,0:T(8,128)S(1)}, f32[32,128]{1,0:T(8,128)}, u32[]{:S(2)}) copy-start(f32[32,128]{1,0:T(8,128)} %k.1) | copy-start | bytes 49156
  2.7 9.4 %copy-start.1 = (f32[90,32,128]{2,1,0:T(8,128)S(1)}, f32[90,32,128]{2,1,0:T(8,128)}, u32[]{:S(2)}) copy-start(f32[90,32,128]{2,1,0:T(8,128)} %t.5) | copy-start | bytes 4423684
  2.7 9.4 %copy-start.7 = (f32[90,512]{1,0:T(8,128)S(1)}, f32[90,512]{1,0:T(8,128)}, u32[]{:S(2)}) copy-start(f32[90,512]{1,0:T(8,128)} %w4.1) | copy-start | bytes 552964
  2.7 9.4 %copy-start.8 = (f32[32,128]{1,0:T(8,128)S(1)}, f32[32,128]{1,0:T(8,128)}, u32[]{:S(2)}) copy-start(f32[32,128]{1,0:T(8,128)} %s.5) | copy-start | bytes 49156
  2.7 9.4 %copy-start.9 = (f32[2,512]{1,0:T(2,128)S(1)}, f32[2,512]{1,0:T(2,128)}, u32[]{:S(2)}) copy-start(f32[2,512]{1,0:T(2,128)} %b2.1) | copy-start | bytes 12292
  2.7 9.4 %copy-start.10 = (f32[512]{0:T(512)S(1)}, f32[512]{0:T(512)}, u32[]{:S(2)}) copy-start(f32[512]{0:T(512)} %param.17) | copy-start | bytes 6148
  2.7 9.4 %copy-start.11 = (f32[90]{0:T(128)S(1)}, f32[90]{0:T(128)}, u32[]{:S(2)}) copy-start(f32[90]{0:T(128)} %param.21) | copy-start | bytes 1084
  4.3 18.1 %collective-permute-start = (f32[192,128]{1,0:T(8,128)S(1)}, f32[192,128]{1,0:T(8,128)S(1)}, u32[]{:S(2)}, u32[]{:S(2)}) collective-permute-start(f32[192,128]{1,0:T(8,128)S(1)} %get-tuple-element.22), channel_id=1, source_target_pairs={{0,1},{1,2},{2,3},{4,5},{5,6},{6,7},{8,9},{9,10},{10,11},{12,13},{... | collective-permute-start | bytes 294920 | tf_op jit(solution)/shard_map/ppermute | solution.py:372
  7.5 14.9 %collective-permute-start.1 = (f32[192,128]{1,0:T(8,128)S(1)}, f32[192,128]{1,0:T(8,128)S(1)}, u32[]{:S(2)}, u32[]{:S(2)}) collective-permute-start(f32[192,128]{1,0:T(8,128)S(1)} %get-tuple-element.23), channel_id=1, source_target_pairs={{1,0},{2,1},{3,2},{5,4},{6,5},{7,6},{9,8},{10,9},{11,10},{13,12},{... | collective-permute-start | bytes 294920 | tf_op jit(solution)/shard_map/ppermute | solution.py:373
  12.2 1.6 %copy-start.4 = (f32[2,512,512]{2,1,0:T(8,128)S(1)}, f32[2,512,512]{2,1,0:T(8,128)}, u32[]{:S(2)}) copy-start(f32[2,512,512]{2,1,0:T(8,128)} %w2.1) | copy-start | bytes 6291460
  13.8 1.4 %copy-start.5 = (f32[90,32,128]{2,1,0:T(8,128)S(1)}, f32[90,32,128]{2,1,0:T(8,128)}, u32[]{:S(2)}) copy-start(f32[90,32,128]{2,1,0:T(8,128)} %m.5) | copy-start | bytes 4423684
  22.5 13.1 %collective-permute-start.3 = (f32[96,128]{1,0:T(8,128)S(1)}, f32[96,128]{1,0:T(8,128)S(1)}, u32[]{:S(2)}, u32[]{:S(2)}) collective-permute-start(f32[96,128]{1,0:T(8,128)S(1)} %get-tuple-element.26.mine_w), channel_id=1, source_target_pairs={{0,252},{4,0},{8,4},{12,8},{16,12},{20,16},{24,20},{28,24},{32,28}... | collective-permute-start | bytes 147464 | tf_op jit(solution)/shard_map/ppermute | solution.py:376
  29.6 6.8 %collective-permute-start.2 = (f32[96,128]{1,0:T(8,128)S(1)}, f32[96,128]{1,0:T(8,128)S(1)}, u32[]{:S(2)}, u32[]{:S(2)}) collective-permute-start(f32[96,128]{1,0:T(8,128)S(1)} %get-tuple-element.27.mine_e), channel_id=1, source_target_pairs={{0,4},{4,8},{8,12},{12,16},{16,20},{20,24},{24,28},{28,32},{32,36}... | collective-permute-start | bytes 147464 | tf_op jit(solution)/shard_map/ppermute | solution.py:377
  29.6 6.8 %copy-start.3 = (f32[32,128]{1,0:T(8,128)S(1)}, f32[32,128]{1,0:T(8,128)}, u32[]{:S(2)}) copy-start(f32[32,128]{1,0:T(8,128)} %k.1) | copy-start | bytes 49156
  29.6 6.8 %copy-start.6 = (f32[90,32,128]{2,1,0:T(8,128)S(1)}, f32[90,32,128]{2,1,0:T(8,128)}, u32[]{:S(2)}) copy-start(f32[90,32,128]{2,1,0:T(8,128)} %m.5) | copy-start | bytes 4423684
where the time goes:
time: 55.1 us; the launch traced here: 54.7 us
  Pallas kernels  33.3 us (60%)
  starting transfers between devices  12.9 us (23%)
  local copies, waits for them, and re-layouts  7 us (13%)
  between operations  0.8 us (1%)
  waiting for transfers between devices  0.79 us (1%)
    pallas_call x1, Pallas kernels, last(): pl.pallas_call(last_kernel, out_shape=(whole, whole), in_specs=[SMEM] + [...  18.3 us
    pallas_call x1, Pallas kernels, first(): pl.pallas_call(first_kernel, out_shape=tuple((jax.ShapeDtypeStruct(*w) fo...  7.24 us
    ppermute x1, starting transfers between devices, on_device(): lax.ppermute(west, 'lon', [(i, (i - 1) % lons) for i in range(lons)])  7.01 us
    unnamed x26, local copies, waits for them, and re-layouts  7 us
    pallas_call x1, Pallas kernels, second(): pl.pallas_call(second_kernel, out_shape=jax.ShapeDtypeStruct(ROW_BLOCK, F...  6.03 us
    ppermute x1, starting transfers between devices, on_device(): north = lax.ppermute(down, 'lat', [(i, i + 1) for i in range(lats - 1)])  3.19 us
    ppermute x1, starting transfers between devices, on_device(): south = lax.ppermute(up, 'lat', [(i + 1, i) for i in range(lats - 1)])  2.65 us
    pallas_call x1, Pallas kernels, pack(): pl.pallas_call(pack_kernel, out_shape=(edge, edge, side, side), in_specs=...  1.59 us
  transfers between devices with their start and end apart: 4, of which 1 were waited for; matrix products, arithmetic and copies ran while one was open for 4% of the time, Pallas kernels for 24%

commit v1 on v0

v1 whole, which is shorter than its diff:
```python
import functools

import jax
import jax.numpy as jnp
from jax import lax
from jax.experimental import pallas as pl
from jax.experimental.pallas import tpu as pltpu
from jax.sharding import PartitionSpec as P

F32 = jnp.float32
BF16 = jnp.bfloat16
F8 = jnp.float8_e4m3fn

LEV = 90
PAD = 96
ROWS = 32
COLS = 128
HID = 512
FEAT = 181
KIN = 2 * PAD
CHUNK = 8
GROUPS = 4
W_LO = 2.0**15
W_HI = 2.0**6
X_LO = 2.0**9
LOAD_LIMIT = 32 << 20

VMEM = pl.BlockSpec(memory_space=pltpu.VMEM)
SMEM = pl.BlockSpec(memory_space=pltpu.SMEM)
HBM = pl.BlockSpec(memory_space=pltpu.HBM)


def split(x):
    hi = x.astype(BF16)
    return hi, (x - hi.astype(F32)).astype(BF16)


def lane_index():
    return lax.broadcasted_iota(jnp.int32, (PAD, COLS), 1)


def put_split(hi_ref, eight_ref, w, n):
    hi = w.astype(BF16)
    hi_ref[...] = hi
    eight_ref[:, 0:n] = ((w - hi.astype(F32)) * W_LO).astype(F8)
    eight_ref[:, n : 2 * n] = (w * W_HI).astype(F8)


def column_of(row, n):
    hi = row.astype(BF16)
    rest = row - hi.astype(F32)
    mid = rest.astype(BF16)
    low = (rest - mid.astype(F32)).astype(BF16)
    parts = jnp.concatenate([hi, mid, low, jnp.zeros((13, n), BF16)], axis=0)
    return lax.dot_general(
        parts, jnp.ones((16, COLS), BF16), (((0,), (0,)), ((), ())), preferred_element_type=F32
    )


def power_below(bound):
    scale = jnp.float32(1.0)
    for k in range(9):
        scale = jnp.where(bound > 440.0 * 2.0**k, scale * 0.5, scale)
    return scale


def put3(dst, w, n):
    hi, lo = split(w)
    dst[:, 0:n] = hi
    dst[:, n : 2 * n] = hi
    dst[:, 2 * n : 3 * n] = lo


def prepare(w1t, b1, w2, b2, w4, b4, w1s, w18, w2s, w28, w4s, bs, sc):
    gap = jnp.zeros((PAD - LEV, HID), F32)
    w1 = jnp.concatenate(
        [w1t[0:LEV], gap, w1t[LEV:FEAT], b1[...], gap[0 : PAD - LEV - 2]], axis=0
    )
    put_split(w1s, w18, jnp.transpose(w1 * 0.5), KIN)
    for k in range(2):
        put_split(w2s.at[k], w28.at[k], w2[k] * 0.5, HID)
    put3(w4s, jnp.concatenate([w4[...], gap], axis=0), HID)
    for k in range(2):
        bs[k * HID : (k + 1) * HID] = column_of(b2[k : k + 1] * 0.5, HID)
    bs[2 * HID : 2 * HID + PAD] = jnp.concatenate(
        [column_of(b4[...], LEV), jnp.zeros((PAD - LEV, COLS), F32)], axis=0
    )
    bound = 6.0 * jnp.max(jnp.sum(jnp.abs(w1), axis=0, keepdims=True))
    sc[0] = power_below(bound)
    bound = bound * jnp.max(jnp.sum(jnp.abs(w2[0]), axis=1, keepdims=True)) + jnp.max(jnp.abs(b2[...]))
    sc[1] = power_below(bound)


def first_columns(block, r, west, east):
    lane = lane_index()
    place = 2 * (r + 1)
    here = (lane == place) | (lane == place + 1)
    rolled = pltpu.roll(block, place, 1) if place else block
    return jnp.where(here, rolled, west), jnp.where(here, pltpu.roll(block, place + 2, 1), east)


def load_kernel(
    t_hbm, m_hbm, s_hbm, k_hbm, w1_hbm, b1_hbm, w2_hbm, b2_hbm, w4_hbm, b4_hbm,
    t, m, w1s, w18, w2s, w28, w4s, bs, sc, up, down, west_out, east_out,
    k, s, w1, b1, w2, b2, w4, b4, sems,
):
    state = [pltpu.make_async_copy(k_hbm, k, sems.at[0])] + [
        pltpu.make_async_copy(t_hbm.at[:, r, :], t.at[r, pl.ds(0, LEV), :], sems.at[0]) for r in range(ROWS)
    ]
    pairs = ((w1_hbm, w1), (b1_hbm, b1), (w2_hbm, w2), (b2_hbm, b2), (w4_hbm, w4), (b4_hbm, b4))
    weights = [pltpu.make_async_copy(a, b, sems.at[1]) for a, b in pairs]
    humid = [pltpu.make_async_copy(s_hbm, s, sems.at[2])] + [
        pltpu.make_async_copy(m_hbm.at[:, r, :], m.at[r, pl.ds(0, LEV), :], sems.at[2]) for r in range(ROWS)
    ]
    for copy in state + weights + humid:
        copy.start()
    for copy in state:
        copy.wait()
    blank = jnp.zeros((PAD - LEV - 1, COLS), F32)
    west = jnp.zeros((PAD, COLS), F32)
    east = jnp.zeros((PAD, COLS), F32)
    for r in range(ROWS):
        t[r, LEV:PAD, :] = jnp.concatenate([k[r : r + 1, :], blank], axis=0)
        west, east = first_columns(t[r], r, west, east)
    west_out[...] = west
    east_out[...] = east
    up[0:PAD] = t[0]
    up[PAD:] = t[1]
    down[0:PAD] = t[ROWS - 1]
    down[PAD:] = t[ROWS - 2]
    for copy in weights:
        copy.wait()
    prepare(w1, b1, w2, b2, w4, b4, w1s, w18, w2s, w28, w4s, bs, sc)
    for copy in humid:
        copy.wait()
    one = jnp.ones((1, COLS), F32)
    for r in range(ROWS):
        m[r, LEV:PAD, :] = jnp.concatenate([s[r : r + 1, :], one, blank[1:]], axis=0)


TRACK = jax.ShapeDtypeStruct((ROWS, PAD, COLS), F32)
EDGE = jax.ShapeDtypeStruct((2 * PAD, COLS), F32)
SIDE = jax.ShapeDtypeStruct((PAD, COLS), F32)
WEIGHTS = (
    ((HID, KIN), BF16),
    ((HID, 2 * KIN), F8),
    ((2, HID, HID), BF16),
    ((2, HID, 2 * HID), F8),
    ((PAD, 3 * HID), BF16),
    ((2 * HID + PAD, COLS), F32),
)


def load(t, m, s, k, w1, b1, w2, b2, w4, b4):
    return pl.pallas_call(
        load_kernel,
        out_shape=(TRACK, TRACK)
        + tuple(jax.ShapeDtypeStruct(*w) for w in WEIGHTS)
        + (jax.ShapeDtypeStruct((2,), F32), EDGE, EDGE, SIDE, SIDE),
        in_specs=[HBM] * 10,
        out_specs=(VMEM,) * 8 + (SMEM,) + (VMEM,) * 4,
        scratch_shapes=[
            pltpu.VMEM((ROWS, COLS), F32),
            pltpu.VMEM((ROWS, COLS), F32),
            pltpu.VMEM((FEAT, HID), F32),
            pltpu.VMEM((1, HID), F32),
            pltpu.VMEM((2, HID, HID), F32),
            pltpu.VMEM((2, HID), F32),
            pltpu.VMEM((LEV, HID), F32),
            pltpu.VMEM((1, LEV), F32),
            pltpu.SemaphoreType.DMA((3,)),
        ],
        compiler_params=pltpu.CompilerParams(vmem_limit_bytes=LOAD_LIMIT),
        cost_estimate=pl.CostEstimate(flops=10**6, bytes_accessed=8 * 10**6, transcendentals=0),
    )(*(pltpu.with_memory_space_constraint(x, pltpu.HBM) for x in (t, m, s, k, w1, b1, w2, b2, w4, b4)))


def corner_kernel(north_ref, south_ref, west_ref, east_ref, w_out, e_out):
    west, east = west_ref[...], east_ref[...]
    west, east = first_columns(north_ref[0:PAD], -1, west, east)
    west, east = first_columns(south_ref[0:PAD], ROWS, west, east)
    w_out[...] = west
    e_out[...] = east


def corners(north, south, west, east):
    side = jax.ShapeDtypeStruct((PAD, COLS), F32)
    return pl.pallas_call(
        corner_kernel,
        out_shape=(side, side),
        in_specs=[VMEM] * 4,
        out_specs=(VMEM, VMEM),
        compiler_params=pltpu.CompilerParams(vmem_limit_bytes=8 << 20),
        cost_estimate=pl.CostEstimate(flops=10**5, bytes_accessed=4 * 10**5, transcendentals=0),
    )(north, south, west, east)


def lit_rows(lit_ref, list_s):
    for r in range(ROWS):
        list_s[r] = 0

    def step(r, carry):
        n, last = carry
        lit = lit_ref[r] > 0

        @pl.when(lit)
        def _():
            list_s[n] = r

        return jnp.where(lit, n + 1, n), jnp.where(lit, r, last)

    n, last = lax.fori_loop(0, ROWS, step, (jnp.int32(0), jnp.int32(0)))

    def fill(i, _):
        list_s[i] = last
        return 0

    lax.fori_loop(n, ROWS, fill, 0)
    return n


def half_silu(u):
    return u + u * jnp.tanh(u)


def dot3(w, x):
    hi, lo = split(x)
    return jnp.dot(w[...], jnp.concatenate([hi, lo, hi], axis=0), preferred_element_type=F32)


def parts8(x, scale):
    hi = x.astype(BF16)
    low = x - hi.astype(F32)
    scaled = x if scale is None else x * scale
    factor = X_LO if scale is None else scale * X_LO
    return hi, jnp.concatenate([scaled.astype(F8), (low * factor).astype(F8)], axis=0)


def dot8(w, w8, held, back):
    hi, eight = held
    v = jnp.dot(w, hi, preferred_element_type=F32)
    return v + jnp.dot(w8, eight, preferred_element_type=F32) * back


def network_chunk(c, list_s, t, m, w1s, w18, w2s, w28, w4s, bs, sc, put):
    rows = [list_s[c * CHUNK + j] for j in range(CHUNK)]
    n = CHUNK // GROUPS
    tile = lambda b: jnp.concatenate([b] * n, axis=1)
    scale = [sc[0], sc[1]]
    back = [1.0 / (W_LO * s) for s in scale]
    held = [None] * GROUPS
    for g in range(GROUPS):
        x = jnp.concatenate(
            [jnp.concatenate([t[r], m[r]], axis=0) for r in rows[g * n : (g + 1) * n]], axis=1
        )
        v = dot8(w1s[...], w18[...], parts8(x, None), 1.0 / W_LO)
        held[g] = parts8(half_silu(v), scale[0])
    for k in range(2):
        for g in range(GROUPS):
            v = dot8(w2s[k], w28[k], held[g], back[k])
            h = half_silu(v + tile(bs[k * HID : (k + 1) * HID]))
            held[g] = parts8(h, scale[1]) if k == 0 else h
    for g in range(GROUPS):
        o = dot3(w4s, held[g]) + tile(bs[2 * HID : 2 * HID + PAD])
        for j in range(n):
            row = rows[g * n + j]
            put(g * n + j, row, o[:, j * COLS : (j + 1) * COLS] * m[row, LEV : LEV + 1, :])


ROW_BLOCK = jax.ShapeDtypeStruct((CHUNK, PAD, COLS), F32)


def some_rows_kernel(c, lit, t, m, w1s, w18, w2s, w28, w4s, bs, sc, out, list_s):
    n = lit_rows(lit, list_s)

    @pl.when(n > c * CHUNK)
    def _():
        def put(j, row, value):
            out[j] = value

        network_chunk(c, list_s, t, m, w1s, w18, w2s, w28, w4s, bs, sc, put)


def some_rows(c, lit, *arrays):
    return pl.pallas_call(
        functools.partial(some_rows_kernel, c),
        out_shape=ROW_BLOCK,
        in_specs=[SMEM] + [VMEM] * 8 + [SMEM],
        out_specs=VMEM,
        scratch_shapes=[pltpu.SMEM((ROWS,), jnp.int32)],
        compiler_params=pltpu.CompilerParams(vmem_limit_bytes=32 << 20),
        cost_estimate=pl.CostEstimate(flops=5 * 10**9, bytes_accessed=8 * 10**6, transcendentals=0),
    )(lit, *arrays)


def last_kernel(
    lit, t, m, w1s, w18, w2s, w28, w4s, bs, sc, heat_a, heat_b, north, south, mine_w, mine_e, west, east,
    heat_hbm, temp_hbm, list_s, heat_s, step_s, temp_s, sems,
):
    n = lit_rows(lit, list_s)

    @pl.when(n < ROWS)
    def _():
        heat_s[...] = jnp.zeros_like(heat_s)

    for part, block in ((0, heat_a), (1, heat_b)):
        @pl.when(n > part * CHUNK)
        def _():
            for j in range(CHUNK):
                heat_s[list_s[part * CHUNK + j]] = block[j]

    def put(j, row, value):
        heat_s[row] = value

    def one(c, _):
        network_chunk(c, list_s, t, m, w1s, w18, w2s, w28, w4s, bs, sc, put)
        return 0

    lax.fori_loop(2, (n + CHUNK - 1) // CHUNK, one, 0)

    def out(src, dst, r, sem):
        return pltpu.make_async_copy(src.at[r, pl.ds(0, LEV), :], dst.at[:, r, :], sem)

    for r in range(ROWS):
        out(heat_s, heat_hbm, r, sems.at[0]).start()

    def state(r):
        if r < 0:
            return north[0:PAD] if r == -1 else north[PAD:]
        if r >= ROWS:
            return south[0:PAD] if r == ROWS else south[PAD:]
        return t[r]

    def number(r):
        if r < 0:
            return north[LEV : LEV + 1]
        if r >= ROWS:
            return south[LEV : LEV + 1]
        return t[r, LEV : LEV + 1, :]

    lane = lane_index()
    odd = lane % 2 == 1
    side = jnp.where(odd, west[...], east[...])

    def compact(far, own, towards):
        near = far[...]
        number = near[LEV : LEV + 1, :]
        around = (
            pltpu.roll(near, 2, 1)
            + pltpu.roll(near, COLS - 2, 1)
            + pltpu.roll(near, towards, 1)
            + pltpu.roll(own[...], towards, 1)
        )
        return near + number * (around - 4.0 * near)

    side_next = jnp.where(odd, compact(west, mine_w, 1), compact(east, mine_e, COLS - 1))
    first_lane, last_lane = lane == 0, lane == COLS - 1

    def substep(above, here, below, number, sides, r):
        edge = pltpu.roll(sides, (-(2 * r + 3)) % COLS, 1)
        left = jnp.where(first_lane, edge, pltpu.roll(here, 1, 1))
        right = jnp.where(last_lane, edge, pltpu.roll(here, COLS - 1, 1))
        return here + number * (above + below + left + right - 4.0 * here)

    for r in range(-1, ROWS + 1):
        step_s[r + 1] = substep(state(r - 1), state(r), state(r + 1), number(r), side, r)
        if r >= 1:
            q = r - 1
            done = substep(step_s[q], step_s[q + 1], step_s[q + 2], number(q), side_next, q)
            temp_s[q] = done + heat_s[q]
            out(temp_s, temp_hbm, q, sems.at[1]).start()
    for r in range(ROWS):
        out(heat_s, heat_hbm, r, sems.at[0]).wait()
    for r in range(ROWS):
        out(temp_s, temp_hbm, r, sems.at[1]).wait()


def last(lit, *arrays):
    whole = jax.ShapeDtypeStruct((LEV, ROWS, COLS), F32)
    track = pltpu.VMEM((ROWS, PAD, COLS), F32)
    return pl.pallas_call(
        last_kernel,
        out_shape=(whole, whole),
        in_specs=[SMEM] + [VMEM] * 8 + [SMEM] + [VMEM] * 8,
        out_specs=(HBM, HBM),
        scratch_shapes=[
            pltpu.SMEM((ROWS,), jnp.int32),
            track,
            pltpu.VMEM((ROWS + 2, PAD, COLS), F32),
            track,
            pltpu.SemaphoreType.DMA((2,)),
        ],
        compiler_params=pltpu.CompilerParams(vmem_limit_bytes=32 << 20),
        cost_estimate=pl.CostEstimate(flops=10**10, bytes_accessed=8 * 10**6, transcendentals=0),
    )(lit, *arrays)


def on_device(t, m, s, lit, k, w1, b1, w2, b2, w4, b4):
    lats, lons = lax.axis_size("lat"), lax.axis_size("lon")
    lit = lit[:, 0]
    t, m, *net, up, down, west, east = load(
        t, m, s, k, w1.T, b1.reshape(1, HID), w2, b2, w4, b4.reshape(1, LEV)
    )
    north = lax.ppermute(down, "lat", [(i, i + 1) for i in range(lats - 1)])
    south = lax.ppermute(up, "lat", [(i + 1, i) for i in range(lats - 1)])
    heat_a = some_rows(0, lit, t, m, *net)
    west, east = corners(north, south, west, east)
    from_east = lax.ppermute(west, "lon", [(i, (i - 1) % lons) for i in range(lons)])
    from_west = lax.ppermute(east, "lon", [(i, (i + 1) % lons) for i in range(lons)])
    heat_b = some_rows(1, lit, t, m, *net)
    return last(lit, t, m, *net, heat_a, heat_b, north, south, west, east, from_west, from_east)


def solution(mesh):
    whole, plane = P(None, "lat", "lon"), P("lat", "lon")
    return jax.shard_map(
        on_device,
        mesh=mesh,
        in_specs=(whole, whole, plane, plane, plane) + (P(),) * 6,
        out_specs=(whole, whole),
        check_vma=False,
    )
```

time: 55.1 us -> 41.8 us (0.76)
  the two profiles are of different devices: /device:TPU:16 before, /device:TPU:8 now
where the time goes in v1:
time: 41.8 us; the launch traced here: 41.7 us
  Pallas kernels  25.7 us (61%)
  starting transfers between devices  12.9 us (31%)
  waiting for transfers between devices  2.24 us (5%)
  between operations  0.88 us (2%)
    pallas_call x1, Pallas kernels, last(): pl.pallas_call(last_kernel, out_shape=(whole, whole), in_specs=[SMEM] + [...  11.9 us
    pallas_call x2, Pallas kernels, some_rows(): pl.pallas_call(functools.partial(some_rows_kernel, c), out_shape=ROW_BLOC...  9.16 us
    ppermute x1, starting transfers between devices, on_device(): lax.ppermute(west, 'lon', [(i, (i - 1) % lons) for i in range(lons)])  7.01 us
    pallas_call x1, Pallas kernels, load(): pl.pallas_call(load_kernel, out_shape=(TRACK, TRACK) + tuple((jax.ShapeDt...  4.48 us
    ppermute x1, starting transfers between devices, on_device(): north = lax.ppermute(down, 'lat', [(i, i + 1) for i in range(lats - 1)])  3.49 us
    ppermute x1, starting transfers between devices, on_device(): south = lax.ppermute(up, 'lat', [(i + 1, i) for i in range(lats - 1)])  2.36 us
    ppermute x1, waiting for transfers between devices, on_device(): lax.ppermute(east, 'lon', [(i, (i + 1) % lons) for i in range(lons)])  2.23 us
  transfers between devices with their start and end apart: 4, of which 1 were waited for; matrix products, arithmetic and copies ran while one was open for 0% of the time, Pallas kernels for 22%

profile of v1, /device:TPU:8, one launch (start us, length us, event | category | flops | bytes accessed | tf_op | source)
XLA Modules:
  0.0 41.7 jit_solution(13203805896615369793)
XLA Ops:
  0.6 0.0 copy-start
  0.6 4.5 %shard_map.122 = (f32[32,96,128]{2,1,0:T(8,128)S(1)}, f32[32,96,128]{2,1,0:T(8,128)S(1)}, bf16[512,192]{1,0:T(8,128)(2,1)S(1)}, f8e4m3fn[512,384]{1,0:T(32,128)(...) custom-call(f32[90,32,128]{2,1,0:T(8,128)} %t_hbm.1, ...), custom_call_target="tpu_custom_call" | custom-call | flops 1000000 | bytes 8000000 | tf_op jit(solution)/shard_map/pallas_call | solution.py:155
  5.1 3.5 %collective-permute-start = (f32[192,128]{1,0:T(8,128)S(1)}, f32[192,128]{1,0:T(8,128)S(1)}, u32[]{:S(2)}, u32[]{:S(2)}) collective-permute-start(f32[192,128]{1,0:T(8,128)S(1)} %get-tuple-element.26), channel_id=1, source_target_pairs={{0,1},{1,2},{2,3},{4,5},{5,6},{6,7},{8,9},{9,10},{10,11},{12,13},{... | collective-permute-start | bytes 294920 | tf_op jit(solution)/shard_map/ppermute | solution.py:404
  8.6 2.4 %collective-permute-start.1 = (f32[192,128]{1,0:T(8,128)S(1)}, f32[192,128]{1,0:T(8,128)S(1)}, u32[]{:S(2)}, u32[]{:S(2)}) collective-permute-start(f32[192,128]{1,0:T(8,128)S(1)} %get-tuple-element.27), channel_id=1, source_target_pairs={{1,0},{2,1},{3,2},{5,4},{6,5},{7,6},{9,8},{10,9},{11,10},{13,12},{... | collective-permute-start | bytes 294920 | tf_op jit(solution)/shard_map/ppermute | solution.py:405
  11.0 0.0 copy-done
  11.0 4.6 %shard_map.124.heat_b = f32[8,96,128]{2,1,0:T(8,128)S(1)} custom-call(s32[32]{0:T(128)S(1)} %bitcast.4, f32[32,96,128]{2,1,0:T(8,128)S(1)} %get-tuple-element.17.t, f32[32,96,128]{2,1,0:T(8,128)S(1)} %get-tuple-element.18.m, bf16[512,192]{1,0:T(8,128)(2,1)S(1)} %get-tuple-element.19.w1s, f8e4m3fn[512,384]{1,0:T(32,128)(4,1)S(1)} %get-tuple-element.20.w18, ...), custom_call_target="tpu_custom_call" | custom-call | flops 5000000000 | bytes 8000000 | tf_op jit(solution)/shard_map/pallas_call | solution.py:285
  15.6 0.0 collective-permute-done.north_ref.north
  15.6 0.0 collective-permute-done.1.south_ref.south
  15.6 0.1 shard_map.125
  15.7 7.0 %collective-permute-start.3 = (f32[96,128]{1,0:T(8,128)S(1)}, f32[96,128]{1,0:T(8,128)S(1)}, u32[]{:S(2)}, u32[]{:S(2)}) collective-permute-start(f32[96,128]{1,0:T(8,128)S(1)} %get-tuple-element.30.mine_w), channel_id=1, source_target_pairs={{0,252},{4,0},{8,4},{12,8},{16,12},{20,16},{24,20},{28,24},{32,28}... | collective-permute-start | bytes 147464 | tf_op jit(solution)/shard_map/ppermute | solution.py:408
  22.7 0.0 collective-permute-start.2
  22.7 4.6 %shard_map.123.heat_a = f32[8,96,128]{2,1,0:T(8,128)S(1)} custom-call(s32[32]{0:T(128)S(1)} %bitcast.5, f32[32,96,128]{2,1,0:T(8,128)S(1)} %get-tuple-element.17.t, f32[32,96,128]{2,1,0:T(8,128)S(1)} %get-tuple-element.18.m, bf16[512,192]{1,0:T(8,128)(2,1)S(1)} %get-tuple-element.19.w1s, f8e4m3fn[512,384]{1,0:T(32,128)(4,1)S(1)} %get-tuple-element.20.w18, ...), custom_call_target="tpu_custom_call" | custom-call | flops 5000000000 | bytes 8000000 | tf_op jit(solution)/shard_map/pallas_call | solution.py:285
  27.3 0.0 collective-permute-done.3.east
  27.3 2.2 %collective-permute-done.2.west = f32[96,128]{1,0:T(8,128)S(1)} collective-permute-done((f32[96,128]{1,0:T(8,128)S(1)}, f32[96,128]{1,0:T(8,128)S(1)}, u32[]{:S(2)}, u32[]{:S(2)}) %collective-permute-start.2) | collective-permute-done | bytes 49184 | tf_op jit(solution)/shard_map/ppermute | solution.py:409
  29.6 11.9 %shard_map.126 = (f32[90,32,128]{2,1,0:T(8,128)}, f32[90,32,128]{2,1,0:T(8,128)}) custom-call(s32[32]{0:T(128)S(1)} %bitcast.6, f32[32,96,128]{2,1,0:T(8,128)S(1)} %get-tuple-element.17.t, f32[32,96,128]{2,1,0:T(8,128)S(1)} %get-tuple-element.18.m, bf16[512,192]{1,0:T(8,128)(2,1)S(1)} %get-tuple-element.19.w1s, ...), custom_call_target="tpu_custom_call" | custom-call | flops 10000000000 | bytes 8000000 | tf_op jit(solution)/shard_map/pallas_call | solution.py:381
Async XLA Ops:
  0.6 10.4 %copy-start = (s32[32,1]{0,1:T(1,128)S(1)}, s32[32,1]{0,1:T(1,128)}, u32[]{:S(2)}) copy-start(s32[32,1]{0,1:T(1,128)} %param.14) | copy-start | bytes 388
  5.1 10.5 %collective-permute-start = (f32[192,128]{1,0:T(8,128)S(1)}, f32[192,128]{1,0:T(8,128)S(1)}, u32[]{:S(2)}, u32[]{:S(2)}) collective-permute-start(f32[192,128]{1,0:T(8,128)S(1)} %get-tuple-element.26), channel_id=1, source_target_pairs={{0,1},{1,2},{2,3},{4,5},{5,6},{6,7},{8,9},{9,10},{10,11},{12,13},{... | collective-permute-start | bytes 294920 | tf_op jit(solution)/shard_map/ppermute | solution.py:404
  8.6 7.0 %collective-permute-start.1 = (f32[192,128]{1,0:T(8,128)S(1)}, f32[192,128]{1,0:T(8,128)S(1)}, u32[]{:S(2)}, u32[]{:S(2)}) collective-permute-start(f32[192,128]{1,0:T(8,128)S(1)} %get-tuple-element.27), channel_id=1, source_target_pairs={{1,0},{2,1},{3,2},{5,4},{6,5},{7,6},{9,8},{10,9},{11,10},{13,12},{... | collective-permute-start | bytes 294920 | tf_op jit(solution)/shard_map/ppermute | solution.py:405
  15.7 11.6 %collective-permute-start.3 = (f32[96,128]{1,0:T(8,128)S(1)}, f32[96,128]{1,0:T(8,128)S(1)}, u32[]{:S(2)}, u32[]{:S(2)}) collective-permute-start(f32[96,128]{1,0:T(8,128)S(1)} %get-tuple-element.30.mine_w), channel_id=1, source_target_pairs={{0,252},{4,0},{8,4},{12,8},{16,12},{20,16},{24,20},{28,24},{32,28}... | collective-permute-start | bytes 147464 | tf_op jit(solution)/shard_map/ppermute | solution.py:408
  22.7 6.8 %collective-permute-start.2 = (f32[96,128]{1,0:T(8,128)S(1)}, f32[96,128]{1,0:T(8,128)S(1)}, u32[]{:S(2)}, u32[]{:S(2)}) collective-permute-start(f32[96,128]{1,0:T(8,128)S(1)} %get-tuple-element.31.mine_e), channel_id=1, source_target_pairs={{0,4},{4,8},{8,12},{12,16},{16,20},{20,24},{24,28},{28,32},{32,36}... | collective-permute-start | bytes 147464 | tf_op jit(solution)/shard_map/ppermute | solution.py:409

commit v2 on v1

v2 whole, which is shorter than its diff:
```python
import functools

import jax
import jax.numpy as jnp
from jax import lax
from jax.experimental import pallas as pl
from jax.experimental.pallas import tpu as pltpu
from jax.sharding import PartitionSpec as P

F32 = jnp.float32
BF16 = jnp.bfloat16
F8 = jnp.float8_e4m3fn

LEV = 90
PAD = 96
ROWS = 32
COLS = 128
HID = 512
FEAT = 181
KIN = 2 * PAD
CHUNK = 8
GROUPS = 4
W_LO = 2.0**15
W_HI = 2.0**6
X_LO = 2.0**9
LOAD_LIMIT = 32 << 20

VMEM = pl.BlockSpec(memory_space=pltpu.VMEM)
HBM = pl.BlockSpec(memory_space=pltpu.HBM)


def split(x):
    hi = x.astype(BF16)
    return hi, (x - hi.astype(F32)).astype(BF16)


def lane_index():
    return lax.broadcasted_iota(jnp.int32, (PAD, COLS), 1)


def put_split(hi_ref, eight_ref, w, n):
    hi = w.astype(BF16)
    hi_ref[...] = hi
    eight_ref[:, 0:n] = ((w - hi.astype(F32)) * W_LO).astype(F8)
    eight_ref[:, n : 2 * n] = (w * W_HI).astype(F8)


def column_of(row, n):
    hi = row.astype(BF16)
    rest = row - hi.astype(F32)
    mid = rest.astype(BF16)
    low = (rest - mid.astype(F32)).astype(BF16)
    parts = jnp.concatenate([hi, mid, low, jnp.zeros((13, n), BF16)], axis=0)
    return lax.dot_general(
        parts, jnp.ones((16, COLS), BF16), (((0,), (0,)), ((), ())), preferred_element_type=F32
    )


def power_below(bound):
    scale = jnp.float32(1.0)
    for k in range(9):
        scale = jnp.where(bound > 440.0 * 2.0**k, 0.5 ** (k + 1), scale)
    return scale


def prepare_outer(w1t, b1, b2, w4, b4, w1s, w18, w4s, bs, sc):
    gap = jnp.zeros((PAD - LEV, HID), F32)
    w1 = jnp.concatenate(
        [w1t[0:LEV], gap, w1t[LEV:FEAT], b1[...], gap[0 : PAD - LEV - 2]], axis=0
    )
    put_split(w1s, w18, jnp.transpose(w1 * 0.5), KIN)
    hi, lo = split(jnp.concatenate([w4[...], gap], axis=0))
    w4s[0:PAD] = hi
    w4s[PAD:] = lo
    for k in range(2):
        bs[k * HID : (k + 1) * HID] = column_of(b2[k : k + 1] * 0.5, HID)
    bs[2 * HID : 2 * HID + PAD] = jnp.concatenate(
        [column_of(b4[...], LEV), jnp.zeros((PAD - LEV, COLS), F32)], axis=0
    )
    bound = 6.0 * jnp.max(jnp.sum(jnp.abs(w1), axis=0, keepdims=True))
    put_scale(sc, 0, bound)
    return bound


def put_scale(sc, k, bound):
    scale = power_below(bound)
    sc[k : k + 1] = jnp.full((1, COLS), scale)
    sc[k + 2 : k + 3] = jnp.full((1, COLS), 1.0 / (W_LO * scale))


def prepare_inner(k, w2, w2s, w28):
    put_split(w2s.at[k], w28.at[k], w2[k] * 0.5, HID)


def first_columns(block, r, west, east):
    lane = lane_index()
    place = 2 * (r + 1)
    here = (lane == place) | (lane == place + 1)
    rolled = pltpu.roll(block, place, 1) if place else block
    return jnp.where(here, rolled, west), jnp.where(here, pltpu.roll(block, place + 2, 1), east)


def load_kernel(
    t_hbm, m_hbm, s_hbm, k_hbm, w1_hbm, b1_hbm, w2_hbm, b2_hbm, w4_hbm, b4_hbm,
    t, m, w1s, w18, w2s, w28, w4s, bs, sc, up, down, west_out, east_out,
    k, s, w1, b1, w2, b2, w4, b4, sems,
):
    def rows(src, dst, sem):
        return [pltpu.make_async_copy(src.at[:, r, :], dst.at[r, pl.ds(0, LEV), :], sem) for r in range(ROWS)]

    pairs = ((w1_hbm, w1), (b1_hbm, b1), (b2_hbm, b2), (w4_hbm, w4), (b4_hbm, b4))
    outer = [pltpu.make_async_copy(a, b, sems.at[0]) for a, b in pairs]
    state = [pltpu.make_async_copy(k_hbm, k, sems.at[1])] + rows(t_hbm, t, sems.at[1])
    inner = [pltpu.make_async_copy(w2_hbm.at[i], w2.at[i], sems.at[2 + i]) for i in range(2)]
    humid = [pltpu.make_async_copy(s_hbm, s, sems.at[4])] + rows(m_hbm, m, sems.at[4])
    for copy in outer + state + inner + humid:
        copy.start()
    for copy in outer:
        copy.wait()
    bound = prepare_outer(w1, b1, b2, w4, b4, w1s, w18, w4s, bs, sc)
    for copy in state:
        copy.wait()
    blank = jnp.zeros((PAD - LEV - 1, COLS), F32)
    west = jnp.zeros((PAD, COLS), F32)
    east = jnp.zeros((PAD, COLS), F32)
    for r in range(ROWS):
        t[r, LEV:PAD, :] = jnp.concatenate([k[r : r + 1, :], blank], axis=0)
        west, east = first_columns(t[r], r, west, east)
    west_out[...] = west
    east_out[...] = east
    up[0:PAD] = t[0]
    up[PAD:] = t[1]
    down[0:PAD] = t[ROWS - 1]
    down[PAD:] = t[ROWS - 2]
    inner[0].wait()
    prepare_inner(0, w2, w2s, w28)
    bound = bound * jnp.max(jnp.sum(jnp.abs(w2[0]), axis=1, keepdims=True)) + jnp.max(jnp.abs(b2[...]))
    put_scale(sc, 1, bound)
    inner[1].wait()
    prepare_inner(1, w2, w2s, w28)
    for copy in humid:
        copy.wait()
    one = jnp.ones((1, COLS), F32)
    for r in range(ROWS):
        m[r, LEV:PAD, :] = jnp.concatenate([s[r : r + 1, :], one, blank[1:]], axis=0)


TRACK = jax.ShapeDtypeStruct((ROWS, PAD, COLS), F32)
EDGE = jax.ShapeDtypeStruct((2 * PAD, COLS), F32)
SIDE = jax.ShapeDtypeStruct((PAD, COLS), F32)
WEIGHTS = (
    ((HID, KIN), BF16),
    ((HID, 2 * KIN), F8),
    ((2, HID, HID), BF16),
    ((2, HID, 2 * HID), F8),
    ((2 * PAD, HID), BF16),
    ((2 * HID + PAD, COLS), F32),
    ((8, COLS), F32),
)


def load(*arrays):
    return pl.pallas_call(
        load_kernel,
        out_shape=(TRACK, TRACK)
        + tuple(jax.ShapeDtypeStruct(*w) for w in WEIGHTS)
        + (EDGE, EDGE, SIDE, SIDE),
        in_specs=[HBM] * 10,
        out_specs=(VMEM,) * 13,
        scratch_shapes=[
            pltpu.VMEM((ROWS, COLS), F32),
            pltpu.VMEM((ROWS, COLS), F32),
            pltpu.VMEM((FEAT, HID), F32),
            pltpu.VMEM((1, HID), F32),
            pltpu.VMEM((2, HID, HID), F32),
            pltpu.VMEM((2, HID), F32),
            pltpu.VMEM((LEV, HID), F32),
            pltpu.VMEM((1, LEV), F32),
            pltpu.SemaphoreType.DMA((5,)),
        ],
        compiler_params=pltpu.CompilerParams(vmem_limit_bytes=LOAD_LIMIT),
        cost_estimate=pl.CostEstimate(flops=10**6, bytes_accessed=8 * 10**6, transcendentals=0),
    )(*(pltpu.with_memory_space_constraint(x, pltpu.HBM) for x in arrays))


def corner_kernel(north_ref, south_ref, west_ref, east_ref, w_out, e_out):
    west, east = west_ref[...], east_ref[...]
    west, east = first_columns(north_ref[0:PAD], -1, west, east)
    west, east = first_columns(south_ref[0:PAD], ROWS, west, east)
    w_out[...] = west
    e_out[...] = east


def corners(north, south, west, east):
    side = jax.ShapeDtypeStruct((PAD, COLS), F32)
    return pl.pallas_call(
        corner_kernel,
        out_shape=(side, side),
        in_specs=[VMEM] * 4,
        out_specs=(VMEM, VMEM),
        compiler_params=pltpu.CompilerParams(vmem_limit_bytes=8 << 20),
        cost_estimate=pl.CostEstimate(flops=10**5, bytes_accessed=4 * 10**5, transcendentals=0),
    )(north, south, west, east)


def all_lit(lit_row):
    return jnp.min(lit_row[...].astype(F32)) > 0.5


def lit_rows(lit_ref, info):
    for r in range(ROWS):
        info[r] = 0

    def step(r, carry):
        n, last = carry
        lit = lit_ref[0, r] > 0

        @pl.when(lit)
        def _():
            info[n] = r

        return jnp.where(lit, n + 1, n), jnp.where(lit, r, last)

    n, last = lax.fori_loop(0, ROWS, step, (jnp.int32(0), jnp.int32(0)))

    def fill(i, _):
        info[i] = last
        return 0

    lax.fori_loop(n, ROWS, fill, 0)
    info[ROWS] = n


def count_lit(lit_row, lit_s, info, sem):
    copy = pltpu.make_async_copy(lit_row, lit_s, sem)
    copy.start()
    copy.wait()
    lit_rows(lit_s, info)
    return info[ROWS]


LIST_SCRATCH = [
    pltpu.SMEM((1, COLS), jnp.int32),
    pltpu.SMEM((ROWS + 8,), jnp.int32),
    pltpu.SemaphoreType.DMA,
]


def half_silu(u):
    return u + u * jnp.tanh(u)


def out_layer(w4s, x):
    hi, lo = split(x)
    both = jnp.dot(w4s[...], hi, preferred_element_type=F32)
    return both[0:PAD] + both[PAD:] + jnp.dot(w4s[0:PAD], lo, preferred_element_type=F32)


def parts8(x, scale):
    hi = x.astype(BF16)
    low = x - hi.astype(F32)
    scaled = x if scale is None else x * scale
    factor = X_LO if scale is None else scale * X_LO
    return hi, jnp.concatenate([scaled.astype(F8), (low * factor).astype(F8)], axis=0)


def dot8(w, w8, held, back):
    hi, eight = held
    v = jnp.dot(w, hi, preferred_element_type=F32)
    return v + jnp.dot(w8, eight, preferred_element_type=F32) * back


def network_chunk(rows, t, m, w1s, w18, w2s, w28, w4s, bs, sc, put, between=lambda: None):
    n = CHUNK // GROUPS
    tile = lambda b: jnp.concatenate([b] * n, axis=1)
    scale = [tile(sc[k : k + 1]) for k in range(2)]
    back = [tile(sc[k : k + 1]) for k in range(2, 4)]
    held = [None] * GROUPS
    for g in range(GROUPS):
        x = jnp.concatenate(
            [jnp.concatenate([t[r], m[r]], axis=0) for r in rows[g * n : (g + 1) * n]], axis=1
        )
        v = dot8(w1s[...], w18[...], parts8(x, None), 1.0 / W_LO)
        held[g] = parts8(half_silu(v), scale[0])
        between()
    for k in range(2):
        for g in range(GROUPS):
            v = dot8(w2s[k], w28[k], held[g], back[k])
            h = half_silu(v + tile(bs[k * HID : (k + 1) * HID]))
            held[g] = parts8(h, scale[1]) if k == 0 else h
            between()
    for g in range(GROUPS):
        o = out_layer(w4s, held[g]) + tile(bs[2 * HID : 2 * HID + PAD])
        for j in range(n):
            row = rows[g * n + j]
            put(g * n + j, row, o[:, j * COLS : (j + 1) * COLS] * m[row, LEV : LEV + 1, :])
        between()


def listed(info, c):
    return [info[c * CHUNK + j] for j in range(CHUNK)]


ROW_BLOCK = jax.ShapeDtypeStruct((CHUNK, PAD, COLS), F32)


def some_rows_kernel(c, lit_row, t, m, w1s, w18, w2s, w28, w4s, bs, sc, out, lit_s, info, sem):
    net = (t, m, w1s, w18, w2s, w28, w4s, bs, sc)
    every = all_lit(lit_row)

    def put(j, row, value):
        out[j] = value

    @pl.when(every)
    def _():
        network_chunk(list(range(c * CHUNK, (c + 1) * CHUNK)), *net, put)

    @pl.when(jnp.logical_not(every))
    def _():
        n = count_lit(lit_row, lit_s, info, sem)

        @pl.when(n > c * CHUNK)
        def _():
            network_chunk(listed(info, c), *net, put)


def some_rows(c, *arrays):
    return pl.pallas_call(
        functools.partial(some_rows_kernel, c),
        out_shape=ROW_BLOCK,
        in_specs=[VMEM] * 10,
        out_specs=VMEM,
        scratch_shapes=LIST_SCRATCH,
        compiler_params=pltpu.CompilerParams(vmem_limit_bytes=32 << 20),
        cost_estimate=pl.CostEstimate(flops=5 * 10**9, bytes_accessed=8 * 10**6, transcendentals=0),
    )(*arrays)


def last_kernel(
    lit_row, t, m, w1s, w18, w2s, w28, w4s, bs, sc, heat_a, heat_b, north, south, mine_w, mine_e, west, east,
    heat_hbm, temp_hbm, lit_s, info, list_sem, heat_s, step_s, temp_s, sems,
):
    net = (t, m, w1s, w18, w2s, w28, w4s, bs, sc)
    every = all_lit(lit_row)

    def heat_out(r, src=None, at=None):
        src, at = (heat_s, r) if src is None else (src, at)
        return pltpu.make_async_copy(src.at[at, pl.ds(0, LEV), :], heat_hbm.at[:, r, :], sems.at[0])

    def temp_out(r):
        return pltpu.make_async_copy(temp_s.at[r, pl.ds(0, LEV), :], temp_hbm.at[:, r, :], sems.at[1])

    def put(j, row, value):
        heat_s[row] = value

    def state(r):
        if r < 0:
            return north[0:PAD] if r == -1 else north[PAD:]
        if r >= ROWS:
            return south[0:PAD] if r == ROWS else south[PAD:]
        return t[r]

    def number(r):
        if r < 0:
            return north[LEV : LEV + 1]
        if r >= ROWS:
            return south[LEV : LEV + 1]
        return t[r, LEV : LEV + 1, :]

    lane = lane_index()
    odd = lane % 2 == 1
    side = jnp.where(odd, west[...], east[...])

    def compact(far, own, towards):
        near = far[...]
        number = near[LEV : LEV + 1, :]
        around = (
            pltpu.roll(near, 2, 1)
            + pltpu.roll(near, COLS - 2, 1)
            + pltpu.roll(near, towards, 1)
            + pltpu.roll(own[...], towards, 1)
        )
        return near + number * (around - 4.0 * near)

    side_next = jnp.where(odd, compact(west, mine_w, 1), compact(east, mine_e, COLS - 1))
    first_lane, last_lane = lane == 0, lane == COLS - 1

    def substep(above, here, below, number, sides, r):
        edge = pltpu.roll(sides, (-(2 * r + 3)) % COLS, 1)
        left = jnp.where(first_lane, edge, pltpu.roll(here, 1, 1))
        right = jnp.where(last_lane, edge, pltpu.roll(here, COLS - 1, 1))
        return here + number * (above + below + left + right - 4.0 * here)

    def step_one(r):
        step_s[r + 1] = substep(state(r - 1), state(r), state(r + 1), number(r), side, r)

    def step_two(r, heat):
        done = substep(step_s[r], step_s[r + 1], step_s[r + 2], number(r), side_next, r)
        temp_s[r] = done + heat
        temp_out(r).start()

    @pl.when(every)
    def _():
        blocks = (heat_a, heat_b)
        early = [heat_out(r, blocks[r // CHUNK], r % CHUNK) for r in range(2 * CHUNK)]
        for copy in early:
            copy.start()
        ahead = iter(range(-1, ROWS + 1))

        def between_one():
            for r in (next(ahead, None), next(ahead, None), next(ahead, None)):
                if r is not None:
                    step_one(r)

        rows = list(range(2 * CHUNK, 3 * CHUNK))
        network_chunk(rows, *net, put, between_one)
        late = [heat_out(r) for r in rows]
        for copy in late:
            copy.start()
        behind = iter(range(3 * CHUNK))

        def between_two():
            for r in (next(behind, None), next(behind, None)):
                if r is not None:
                    step_two(r, blocks[r // CHUNK][r % CHUNK] if r < 2 * CHUNK else heat_s[r])

        rows = list(range(3 * CHUNK, ROWS))
        network_chunk(rows, *net, put, between_two)
        for r in rows:
            copy = heat_out(r)
            copy.start()
            late.append(copy)
            step_two(r, heat_s[r])
        for copy in early + late:
            copy.wait()
        for r in range(ROWS):
            temp_out(r).wait()

    @pl.when(jnp.logical_not(every))
    def _():
        n = count_lit(lit_row, lit_s, info, list_sem)
        heat_s[...] = jnp.zeros_like(heat_s)
        for part, block in ((0, heat_a), (1, heat_b)):
            @pl.when(n > part * CHUNK)
            def _():
                for j in range(CHUNK):
                    heat_s[info[part * CHUNK + j]] = block[j]

        def one(c, _):
            network_chunk(listed(info, c), *net, put)
            return 0

        lax.fori_loop(2, (n + CHUNK - 1) // CHUNK, one, 0)
        for r in range(ROWS):
            heat_out(r).start()
        for r in range(-1, ROWS + 1):
            step_one(r)
            if r >= 1:
                step_two(r - 1, heat_s[r - 1])
        for r in range(ROWS):
            heat_out(r).wait()
        for r in range(ROWS):
            temp_out(r).wait()


def last(*arrays):
    whole = jax.ShapeDtypeStruct((LEV, ROWS, COLS), F32)
    track = pltpu.VMEM((ROWS, PAD, COLS), F32)
    return pl.pallas_call(
        last_kernel,
        out_shape=(whole, whole),
        in_specs=[VMEM] * 18,
        out_specs=(HBM, HBM),
        scratch_shapes=LIST_SCRATCH
        + [
            track,
            pltpu.VMEM((ROWS + 2, PAD, COLS), F32),
            track,
            pltpu.SemaphoreType.DMA((2,)),
        ],
        compiler_params=pltpu.CompilerParams(vmem_limit_bytes=32 << 20),
        cost_estimate=pl.CostEstimate(flops=10**10, bytes_accessed=8 * 10**6, transcendentals=0),
    )(*arrays)


def on_device(t, m, s, lit, k, w1, b1, w2, b2, w4, b4):
    lats, lons = lax.axis_size("lat"), lax.axis_size("lon")
    lit_row = jnp.concatenate([lit.reshape(1, ROWS), jnp.ones((1, COLS - ROWS), jnp.int32)], axis=1)
    t, m, *net, up, down, west, east = load(
        t, m, s, k, w1.T, b1.reshape(1, HID), w2, b2, w4, b4.reshape(1, LEV)
    )
    north = lax.ppermute(down, "lat", [(i, i + 1) for i in range(lats - 1)])
    south = lax.ppermute(up, "lat", [(i + 1, i) for i in range(lats - 1)])
    heat_a = some_rows(0, lit_row, t, m, *net)
    west, east = corners(north, south, west, east)
    from_east = lax.ppermute(west, "lon", [(i, (i - 1) % lons) for i in range(lons)])
    from_west = lax.ppermute(east, "lon", [(i, (i + 1) % lons) for i in range(lons)])
    heat_b = some_rows(1, lit_row, t, m, *net)
    return last(lit_row, t, m, *net, heat_a, heat_b, north, south, west, east, from_west, from_east)


def solution(mesh):
    whole, plane = P(None, "lat", "lon"), P("lat", "lon")
    return jax.shard_map(
        on_device,
        mesh=mesh,
        in_specs=(whole, whole, plane, plane, plane) + (P(),) * 6,
        out_specs=(whole, whole),
        check_vma=False,
    )
```

time: 41.8 us -> 37.8 us (0.904)
  Pallas kernels: 25.7 us -> 21 us
  waiting for transfers between devices: 2.24 us -> 3.31 us
    pallas_call x1, Pallas kernels: 11.9 us -> 9.49 us  [last(): pl.pallas_call(last_kernel, out_shape=(whole, whole), in_specs=[VMEM] * 1...]
    pallas_call x2, Pallas kernels: 9.16 us -> 7.61 us  [some_rows(): pl.pallas_call(functools.partial(some_rows_kernel, c), out_shape=ROW_BLOC...]
    pallas_call x1, Pallas kernels: 4.48 us -> 3.75 us  [load(): pl.pallas_call(load_kernel, out_shape=(TRACK, TRACK) + tuple((jax.ShapeDt...]
    ppermute x1, waiting for transfers between devices: 2.23 us -> 2.92 us  [on_device(): lax.ppermute(east, 'lon', [(i, (i + 1) % lons) for i in range(lons)])]
  transfers between devices with their start and end apart: 4 -> 4, of which waited for: 1 -> 2; matrix products, arithmetic and copies ran while one was open for 0% -> 0% of each run, Pallas kernels for 22% -> 20%
where the time goes in v2:
time: 37.8 us; the launch traced here: 37.7 us
  Pallas kernels  21 us (56%)
  starting transfers between devices  12.5 us (33%)
  waiting for transfers between devices  3.31 us (9%)
  between operations  0.9 us (2%)
    pallas_call x1, Pallas kernels, last(): pl.pallas_call(last_kernel, out_shape=(whole, whole), in_specs=[VMEM] * 1...  9.49 us
    pallas_call x2, Pallas kernels, some_rows(): pl.pallas_call(functools.partial(some_rows_kernel, c), out_shape=ROW_BLOC...  7.61 us
    ppermute x1, starting transfers between devices, on_device(): lax.ppermute(west, 'lon', [(i, (i - 1) % lons) for i in range(lons)])  6.64 us
    pallas_call x1, Pallas kernels, load(): pl.pallas_call(load_kernel, out_shape=(TRACK, TRACK) + tuple((jax.ShapeDt...  3.75 us
    ppermute x1, starting transfers between devices, on_device(): north = lax.ppermute(down, 'lat', [(i, i + 1) for i in range(lats - 1)])  3.48 us
    ppermute x1, waiting for transfers between devices, on_device(): lax.ppermute(east, 'lon', [(i, (i + 1) % lons) for i in range(lons)])  2.92 us
    ppermute x1, starting transfers between devices, on_device(): south = lax.ppermute(up, 'lat', [(i + 1, i) for i in range(lats - 1)])  2.36 us
  transfers between devices with their start and end apart: 4, of which 2 were waited for; matrix products, arithmetic and copies ran while one was open for 0% of the time, Pallas kernels for 20%

profile of v2, /device:TPU:8, one launch (start us, length us, event | category | flops | bytes accessed | tf_op | source)
XLA Modules:
  0.0 37.7 jit_solution(10162610788182355519)
XLA Ops:
  0.6 0.0 copy-start
  0.6 3.8 %shard_map.122 = (f32[32,96,128]{2,1,0:T(8,128)S(1)}, f32[32,96,128]{2,1,0:T(8,128)S(1)}, bf16[512,192]{1,0:T(8,128)(2,1)S(1)}, f8e4m3fn[512,384]{1,0:T(32,128)(...) custom-call(f32[90,32,128]{2,1,0:T(8,128)} %t_hbm.1, ...), custom_call_target="tpu_custom_call" | custom-call | flops 1000000 | bytes 8000000 | tf_op jit(solution)/shard_map/pallas_call | solution.py:163
  4.4 3.5 %collective-permute-start = (f32[192,128]{1,0:T(8,128)S(1)}, f32[192,128]{1,0:T(8,128)S(1)}, u32[]{:S(2)}, u32[]{:S(2)}) collective-permute-start(f32[192,128]{1,0:T(8,128)S(1)} %get-tuple-element.26), channel_id=1, source_target_pairs={{0,1},{1,2},{2,3},{4,5},{5,6},{6,7},{8,9},{9,10},{10,11},{12,13},{... | collective-permute-start | bytes 294920 | tf_op jit(solution)/shard_map/ppermute | solution.py:492
  7.9 2.4 %collective-permute-start.1 = (f32[192,128]{1,0:T(8,128)S(1)}, f32[192,128]{1,0:T(8,128)S(1)}, u32[]{:S(2)}, u32[]{:S(2)}) collective-permute-start(f32[192,128]{1,0:T(8,128)S(1)} %get-tuple-element.27), channel_id=1, source_target_pairs={{1,0},{2,1},{3,2},{5,4},{6,5},{7,6},{9,8},{10,9},{11,10},{13,12},{... | collective-permute-start | bytes 294920 | tf_op jit(solution)/shard_map/ppermute | solution.py:493
  10.3 0.0 copy-done
  10.3 3.7 %shard_map.124.heat_b = f32[8,96,128]{2,1,0:T(8,128)S(1)} custom-call(s32[1,128]{1,0:T(1,128)S(1)} %concatenate.3.lit_row, f32[32,96,128]{2,1,0:T(8,128)S(1)} %get-tuple-element.17.t, f32[32,96,128]{2,1,0:T(8,128)S(1)} %get-tuple-element.18.m, bf16[512,192]{1,0:T(8,128)(2,1)S(1)} %get-tuple-element.19.w1s, f8e4m3fn[512,384]{1,0:T(32,128)(4,1)S(1)} %get-tuple-element.20.w18, ...), custom_call_target="tpu_custom_call" | custom-call | flops 5000000000 | bytes 8000000 | tf_op jit(solution)/shard_map/pallas_call | solution.py:328
  14.0 0.0 collective-permute-done.north_ref.north
  14.0 0.4 %collective-permute-done.1.south_ref.south = f32[192,128]{1,0:T(8,128)S(1)} collective-permute-done((f32[192,128]{1,0:T(8,128)S(1)}, f32[192,128]{1,0:T(8,128)S(1)}, u32[]{:S(2)}, u32[]{:S(2)}) %collective-permute-start.1) | collective-permute-done | bytes 98336 | tf_op jit(solution)/shard_map/ppermute | solution.py:493
  14.4 0.1 shard_map.125
  14.5 6.6 %collective-permute-start.3 = (f32[96,128]{1,0:T(8,128)S(1)}, f32[96,128]{1,0:T(8,128)S(1)}, u32[]{:S(2)}, u32[]{:S(2)}) collective-permute-start(f32[96,128]{1,0:T(8,128)S(1)} %get-tuple-element.30.mine_w), channel_id=1, source_target_pairs={{0,252},{4,0},{8,4},{12,8},{16,12},{20,16},{24,20},{28,24},{32,28}... | collective-permute-start | bytes 147464 | tf_op jit(solution)/shard_map/ppermute | solution.py:496
  21.1 0.0 collective-permute-start.2
  21.2 3.9 %shard_map.123.heat_a = f32[8,96,128]{2,1,0:T(8,128)S(1)} custom-call(s32[1,128]{1,0:T(1,128)S(1)} %concatenate.3.lit_row, f32[32,96,128]{2,1,0:T(8,128)S(1)} %get-tuple-element.17.t, f32[32,96,128]{2,1,0:T(8,128)S(1)} %get-tuple-element.18.m, bf16[512,192]{1,0:T(8,128)(2,1)S(1)} %get-tuple-element.19.w1s, f8e4m3fn[512,384]{1,0:T(32,128)(4,1)S(1)} %get-tuple-element.20.w18, ...), custom_call_target="tpu_custom_call" | custom-call | flops 5000000000 | bytes 8000000 | tf_op jit(solution)/shard_map/pallas_call | solution.py:328
  25.1 0.0 collective-permute-done.3.east
  25.1 2.9 %collective-permute-done.2.west = f32[96,128]{1,0:T(8,128)S(1)} collective-permute-done((f32[96,128]{1,0:T(8,128)S(1)}, f32[96,128]{1,0:T(8,128)S(1)}, u32[]{:S(2)}, u32[]{:S(2)}) %collective-permute-start.2) | collective-permute-done | bytes 49184 | tf_op jit(solution)/shard_map/ppermute | solution.py:497
  28.0 9.5 %shard_map.126 = (f32[90,32,128]{2,1,0:T(8,128)}, f32[90,32,128]{2,1,0:T(8,128)}) custom-call(s32[1,128]{1,0:T(1,128)S(1)} %concatenate.3.lit_row, f32[32,96,128]{2,1,0:T(8,128)S(1)} %get-tuple-element.17.t, f32[32,96,128]{2,1,0:T(8,128)S(1)} %get-tuple-element.18.m, bf16[512,192]{1,0:T(8,128)(2,1)S(1)} %get-tuple-element.19.w1s, ...), custom_call_target="tpu_custom_call" | custom-call | flops 10000000000 | bytes 8000000 | tf_op jit(solution)/shard_map/pallas_call | solution.py:469
  (1 shorter events, 0.0 us)
Async XLA Ops:
  0.6 9.6 %copy-start = (s32[32,1]{0,1:T(1,128)S(1)}, s32[32,1]{0,1:T(1,128)}, u32[]{:S(2)}) copy-start(s32[32,1]{0,1:T(1,128)} %param.14) | copy-start | bytes 388
  4.4 9.6 %collective-permute-start = (f32[192,128]{1,0:T(8,128)S(1)}, f32[192,128]{1,0:T(8,128)S(1)}, u32[]{:S(2)}, u32[]{:S(2)}) collective-permute-start(f32[192,128]{1,0:T(8,128)S(1)} %get-tuple-element.26), channel_id=1, source_target_pairs={{0,1},{1,2},{2,3},{4,5},{5,6},{6,7},{8,9},{9,10},{10,11},{12,13},{... | collective-permute-start | bytes 294920 | tf_op jit(solution)/shard_map/ppermute | solution.py:492
  7.9 6.5 %collective-permute-start.1 = (f32[192,128]{1,0:T(8,128)S(1)}, f32[192,128]{1,0:T(8,128)S(1)}, u32[]{:S(2)}, u32[]{:S(2)}) collective-permute-start(f32[192,128]{1,0:T(8,128)S(1)} %get-tuple-element.27), channel_id=1, source_target_pairs={{1,0},{2,1},{3,2},{5,4},{6,5},{7,6},{9,8},{10,9},{11,10},{13,12},{... | collective-permute-start | bytes 294920 | tf_op jit(solution)/shard_map/ppermute | solution.py:493
  14.5 10.5 %collective-permute-start.3 = (f32[96,128]{1,0:T(8,128)S(1)}, f32[96,128]{1,0:T(8,128)S(1)}, u32[]{:S(2)}, u32[]{:S(2)}) collective-permute-start(f32[96,128]{1,0:T(8,128)S(1)} %get-tuple-element.30.mine_w), channel_id=1, source_target_pairs={{0,252},{4,0},{8,4},{12,8},{16,12},{20,16},{24,20},{28,24},{32,28}... | collective-permute-start | bytes 147464 | tf_op jit(solution)/shard_map/ppermute | solution.py:496
  21.1 6.8 %collective-permute-start.2 = (f32[96,128]{1,0:T(8,128)S(1)}, f32[96,128]{1,0:T(8,128)S(1)}, u32[]{:S(2)}, u32[]{:S(2)}) collective-permute-start(f32[96,128]{1,0:T(8,128)S(1)} %get-tuple-element.31.mine_e), channel_id=1, source_target_pairs={{0,4},{4,8},{8,12},{12,16},{16,20},{20,24},{24,28},{28,32},{32,36}... | collective-permute-start | bytes 147464 | tf_op jit(solution)/shard_map/ppermute | solution.py:497

commit v3 on v2

v3 whole, which is shorter than its diff:
```python
import functools

import jax
import jax.numpy as jnp
from jax import lax
from jax.experimental import pallas as pl
from jax.experimental.pallas import tpu as pltpu
from jax.sharding import PartitionSpec as P

F32 = jnp.float32
BF16 = jnp.bfloat16
F8 = jnp.float8_e4m3fn

LEV = 90
PAD = 96
ROWS = 32
COLS = 128
HID = 512
FEAT = 181
KIN = 2 * PAD
CHUNK = 8
GROUPS = 4
W_LO = 2.0**15
W_HI = 2.0**6
X_LO = 2.0**9
NET_LIMIT = 32 << 20

VMEM = pl.BlockSpec(memory_space=pltpu.VMEM)
HBM = pl.BlockSpec(memory_space=pltpu.HBM)


def split(x):
    hi = x.astype(BF16)
    return hi, (x - hi.astype(F32)).astype(BF16)


def lane_index():
    return lax.broadcasted_iota(jnp.int32, (PAD, COLS), 1)


def put_split(hi_ref, eight_ref, w, n):
    hi = w.astype(BF16)
    hi_ref[...] = hi
    eight_ref[:, 0:n] = ((w - hi.astype(F32)) * W_LO).astype(F8)
    eight_ref[:, n : 2 * n] = (w * W_HI).astype(F8)


def column_of(row, n):
    hi = row.astype(BF16)
    rest = row - hi.astype(F32)
    mid = rest.astype(BF16)
    low = (rest - mid.astype(F32)).astype(BF16)
    parts = jnp.concatenate([hi, mid, low, jnp.zeros((13, n), BF16)], axis=0)
    return lax.dot_general(
        parts, jnp.ones((16, COLS), BF16), (((0,), (0,)), ((), ())), preferred_element_type=F32
    )


def power_below(bound):
    scale = jnp.float32(1.0)
    for k in range(9):
        scale = jnp.where(bound > 440.0 * 2.0**k, 0.5 ** (k + 1), scale)
    return scale


def prepare_outer(w1t, b1, b2, w4, b4, w1s, w18, w4s, bs, sc):
    gap = jnp.zeros((PAD - LEV, HID), F32)
    w1 = jnp.concatenate(
        [w1t[0:LEV], gap, w1t[LEV:FEAT], b1[...], gap[0 : PAD - LEV - 2]], axis=0
    )
    put_split(w1s, w18, jnp.transpose(w1 * 0.5), KIN)
    hi, lo = split(jnp.concatenate([w4[...], gap], axis=0))
    w4s[0:PAD] = hi
    w4s[PAD:] = lo
    for k in range(2):
        bs[k * HID : (k + 1) * HID] = column_of(b2[k : k + 1] * 0.5, HID)
    bs[2 * HID : 2 * HID + PAD] = jnp.concatenate(
        [column_of(b4[...], LEV), jnp.zeros((PAD - LEV, COLS), F32)], axis=0
    )
    bound = 6.0 * jnp.max(jnp.sum(jnp.abs(w1), axis=0, keepdims=True))
    put_scale(sc, 0, bound)
    return bound


def put_scale(sc, k, bound):
    scale = power_below(bound)
    sc[k : k + 1] = jnp.full((1, COLS), scale)
    sc[k + 2 : k + 3] = jnp.full((1, COLS), 1.0 / (W_LO * scale))


def prepare_inner(k, w2, w2s, w28):
    put_split(w2s.at[k], w28.at[k], w2[k] * 0.5, HID)


def first_columns(block, r, west, east):
    lane = lane_index()
    place = 2 * (r + 1)
    here = (lane == place) | (lane == place + 1)
    rolled = pltpu.roll(block, place, 1) if place else block
    return jnp.where(here, rolled, west), jnp.where(here, pltpu.roll(block, place + 2, 1), east)


def rows_in(src, dst, sem):
    return [pltpu.make_async_copy(src.at[:, r, :], dst.at[r, pl.ds(0, LEV), :], sem) for r in range(ROWS)]


def pack_kernel(t_hbm, k_hbm, t, pay_a, pay_b, west_out, east_out, k, sem):
    copies = [pltpu.make_async_copy(k_hbm, k, sem)] + rows_in(t_hbm, t, sem)
    for copy in copies:
        copy.start()
    pay_b[PAD:] = jnp.zeros((PAY_B - PAD, COLS), F32)
    for copy in copies:
        copy.wait()
    blank = jnp.zeros((PAD - LEV - 1, COLS), F32)
    west = jnp.zeros((PAD, COLS), F32)
    east = jnp.zeros((PAD, COLS), F32)
    for r in range(ROWS):
        t[r, LEV:PAD, :] = jnp.concatenate([k[r : r + 1, :], blank], axis=0)
        west, east = first_columns(t[r], r, west, east)
    west_out[...] = west
    east_out[...] = east
    for i, r in enumerate((ROWS - 1, ROWS - 2, 0, 1)):
        pay_a[i * PAD : (i + 1) * PAD] = t[r]
    even = lax.axis_index("lon") % 2 == 0
    pay_a[4 * PAD : 5 * PAD] = jnp.where(even, east, west)
    pay_b[0:PAD] = jnp.where(even, west, east)


def in_hbm(*arrays):
    return [pltpu.with_memory_space_constraint(x, pltpu.HBM) for x in arrays]


TRACK = jax.ShapeDtypeStruct((ROWS, PAD, COLS), F32)
PAY_A = 5 * PAD
PAY_B = 256
SIDE = jax.ShapeDtypeStruct((PAD, COLS), F32)
def pack(t, k):
    return pl.pallas_call(
        pack_kernel,
        out_shape=(
            TRACK,
            jax.ShapeDtypeStruct((PAY_A, COLS), F32),
            jax.ShapeDtypeStruct((PAY_B, COLS), F32),
            SIDE,
            SIDE,
        ),
        in_specs=[HBM] * 2,
        out_specs=(VMEM,) * 5,
        scratch_shapes=[pltpu.VMEM((ROWS, COLS), F32), pltpu.SemaphoreType.DMA],
        compiler_params=pltpu.CompilerParams(vmem_limit_bytes=16 << 20),
        cost_estimate=pl.CostEstimate(flops=10**6, bytes_accessed=4 * 10**6, transcendentals=0),
    )(*in_hbm(t, k))


def all_lit(lit_row):
    return jnp.min(lit_row[...].astype(F32)) > 0.5


def lit_rows(lit_ref, info):
    for r in range(ROWS):
        info[r] = 0

    def step(r, carry):
        n, last = carry
        lit = lit_ref[0, r] > 0

        @pl.when(lit)
        def _():
            info[n] = r

        return jnp.where(lit, n + 1, n), jnp.where(lit, r, last)

    n, last = lax.fori_loop(0, ROWS, step, (jnp.int32(0), jnp.int32(0)))

    def fill(i, _):
        info[i] = last
        return 0

    lax.fori_loop(n, ROWS, fill, 0)
    info[ROWS] = n


def count_lit(lit_row, lit_s, info, sem):
    copy = pltpu.make_async_copy(lit_row, lit_s, sem)
    copy.start()
    copy.wait()
    lit_rows(lit_s, info)
    return info[ROWS]


LIST_SCRATCH = [
    pltpu.SMEM((1, COLS), jnp.int32),
    pltpu.SMEM((ROWS + 8,), jnp.int32),
    pltpu.SemaphoreType.DMA,
]


def half_silu(u):
    return u + u * jnp.tanh(u)


def out_layer(w4s, x):
    hi, lo = split(x)
    both = jnp.dot(w4s[...], hi, preferred_element_type=F32)
    return both[0:PAD] + both[PAD:] + jnp.dot(w4s[0:PAD], lo, preferred_element_type=F32)


def parts8(x, scale):
    hi = x.astype(BF16)
    low = x - hi.astype(F32)
    scaled = x if scale is None else x * scale
    factor = X_LO if scale is None else scale * X_LO
    return hi, jnp.concatenate([scaled.astype(F8), (low * factor).astype(F8)], axis=0)


def dot8(w, w8, held, back):
    hi, eight = held
    v = jnp.dot(w, hi, preferred_element_type=F32)
    return v + jnp.dot(w8, eight, preferred_element_type=F32) * back


def network_chunk(rows, t, m, w1s, w18, w2s, w28, w4s, bs, sc, put, between=lambda: None):
    n = CHUNK // GROUPS
    tile = lambda b: jnp.concatenate([b] * n, axis=1)
    scale = [tile(sc[k : k + 1]) for k in range(2)]
    back = [tile(sc[k : k + 1]) for k in range(2, 4)]
    held = [None] * GROUPS
    for g in range(GROUPS):
        x = jnp.concatenate(
            [jnp.concatenate([t[r], m[r]], axis=0) for r in rows[g * n : (g + 1) * n]], axis=1
        )
        v = dot8(w1s[...], w18[...], parts8(x, None), 1.0 / W_LO)
        held[g] = parts8(half_silu(v), scale[0])
        between()
    for k in range(2):
        for g in range(GROUPS):
            v = dot8(w2s[k], w28[k], held[g], back[k])
            h = half_silu(v + tile(bs[k * HID : (k + 1) * HID]))
            held[g] = parts8(h, scale[1]) if k == 0 else h
            between()
    for g in range(GROUPS):
        o = out_layer(w4s, held[g]) + tile(bs[2 * HID : 2 * HID + PAD])
        for j in range(n):
            row = rows[g * n + j]
            put(g * n + j, row, o[:, j * COLS : (j + 1) * COLS] * m[row, LEV : LEV + 1, :])
        between()


def listed(info, c):
    return [info[c * CHUNK + j] for j in range(CHUNK)]


def heat_kernel(
    lit_row, t, m_hbm, s_hbm, w1_hbm, b1_hbm, w2_hbm, b2_hbm, w4_hbm, b4_hbm, heat,
    m, w1s, w18, w2s, w28, w4s, bs, sc, s, w1, b1, w2, b2, w4, b4, lit_s, info, sem, sems,
):
    every = all_lit(lit_row)
    pairs = ((w1_hbm, w1), (b1_hbm, b1), (b2_hbm, b2), (w4_hbm, w4), (b4_hbm, b4))
    outer = [pltpu.make_async_copy(a, b, sems.at[0]) for a, b in pairs]
    inner = [pltpu.make_async_copy(w2_hbm.at[i], w2.at[i], sems.at[1 + i]) for i in range(2)]
    humid = [pltpu.make_async_copy(s_hbm, s, sems.at[3])] + rows_in(m_hbm, m, sems.at[3])
    for copy in outer + inner + humid:
        copy.start()

    @pl.when(every)
    def _():
        for r in range(ROWS):
            info[r] = r
        info[ROWS] = ROWS

    @pl.when(jnp.logical_not(every))
    def _():
        count_lit(lit_row, lit_s, info, sem)
        heat[...] = jnp.zeros_like(heat)

    for copy in outer:
        copy.wait()
    bound = prepare_outer(w1, b1, b2, w4, b4, w1s, w18, w4s, bs, sc)
    inner[0].wait()
    prepare_inner(0, w2, w2s, w28)
    bound = bound * jnp.max(jnp.sum(jnp.abs(w2[0]), axis=1, keepdims=True)) + jnp.max(jnp.abs(b2[...]))
    put_scale(sc, 1, bound)
    inner[1].wait()
    prepare_inner(1, w2, w2s, w28)
    for copy in humid:
        copy.wait()
    last_levels = jnp.concatenate([jnp.ones((1, COLS), F32), jnp.zeros((PAD - LEV - 2, COLS), F32)], axis=0)
    for r in range(ROWS):
        m[r, LEV:PAD, :] = jnp.concatenate([s[r : r + 1, :], last_levels], axis=0)

    def put(j, row, value):
        heat[row] = value

    def one(c, _):
        network_chunk(listed(info, c), t, m, w1s, w18, w2s, w28, w4s, bs, sc, put)
        return 0

    lax.fori_loop(0, (info[ROWS] + CHUNK - 1) // CHUNK, one, 0)


WEIGHTS = (
    ((HID, KIN), BF16),
    ((HID, 2 * KIN), F8),
    ((2, HID, HID), BF16),
    ((2, HID, 2 * HID), F8),
    ((2 * PAD, HID), BF16),
    ((2 * HID + PAD, COLS), F32),
    ((8, COLS), F32),
)


def heat_of(lit_row, t, *arrays):
    return pl.pallas_call(
        heat_kernel,
        out_shape=TRACK,
        in_specs=[VMEM] * 2 + [HBM] * 8,
        out_specs=VMEM,
        scratch_shapes=[pltpu.VMEM((ROWS, PAD, COLS), F32)]
        + [pltpu.VMEM(*shape) for shape in WEIGHTS]
        + [
            pltpu.VMEM((ROWS, COLS), F32),
            pltpu.VMEM((FEAT, HID), F32),
            pltpu.VMEM((1, HID), F32),
            pltpu.VMEM((2, HID, HID), F32),
            pltpu.VMEM((2, HID), F32),
            pltpu.VMEM((LEV, HID), F32),
            pltpu.VMEM((1, LEV), F32),
        ]
        + LIST_SCRATCH
        + [pltpu.SemaphoreType.DMA((4,))],
        compiler_params=pltpu.CompilerParams(vmem_limit_bytes=NET_LIMIT),
        cost_estimate=pl.CostEstimate(flops=2 * 10**10, bytes_accessed=8 * 10**6, transcendentals=0),
    )(lit_row, t, *in_hbm(*arrays))


def diffuse_kernel(
    t, heat, gather_a, gather_b, mine_w, mine_e, heat_hbm, temp_hbm, edges, sides, step_s, temp_s, sems,
):
    lat, lats = lax.axis_index("lat"), lax.axis_size("lat")
    even = lax.axis_index("lon") % 2 == 0
    above, below = jnp.maximum(lat - 1, 0), jnp.minimum(lat + 1, lats - 1)
    mine = jnp.where(even, 0, lats)
    other = lats - mine

    def fetch(src, place, start, count, dst):
        return pltpu.make_async_copy(src.at[place, pl.ds(start, count)], dst, sems.at[0])

    copies = [
        fetch(gather_a, mine + above, 0, 2 * PAD, edges.at[0]),
        fetch(gather_a, mine + below, 2 * PAD, 2 * PAD, edges.at[1]),
    ]
    for i, row in enumerate((above, lat, below)):
        copies.append(fetch(gather_a, other + row, 4 * PAD, PAD, sides.at[i]))
        copies.append(fetch(gather_b, mine + row, 0, PAD, sides.at[3 + i]))
    for copy in copies:
        copy.start()

    def heat_out(r):
        return pltpu.make_async_copy(heat.at[r, pl.ds(0, LEV), :], heat_hbm.at[:, r, :], sems.at[1])

    def temp_out(r):
        return pltpu.make_async_copy(temp_s.at[r, pl.ds(0, LEV), :], temp_hbm.at[:, r, :], sems.at[2])

    for r in range(ROWS):
        heat_out(r).start()
    for copy in copies:
        copy.wait()
    lane = lane_index()
    top = jnp.where(lat > 0, 1.0, 0.0).astype(F32)
    bottom = jnp.where(lat < lats - 1, 1.0, 0.0).astype(F32)
    edges[0] = edges[0] * top
    edges[1] = edges[1] * bottom

    def column(i):
        before = pltpu.roll(sides[i], COLS // 2, 1) * top
        after = pltpu.roll(sides[i + 2], COLS // 2, 1) * bottom
        return jnp.where(lane < 2, before, jnp.where(lane < 2 * (ROWS + 1), sides[i + 1], after))

    in_a, in_b = column(0), column(3)
    west, east = jnp.where(even, in_b, in_a), jnp.where(even, in_a, in_b)

    def state(r):
        if r < 0:
            return edges[0, 0:PAD] if r == -1 else edges[0, PAD : 2 * PAD]
        if r >= ROWS:
            return edges[1, 0:PAD] if r == ROWS else edges[1, PAD : 2 * PAD]
        return t[r]

    def number(r):
        if r < 0:
            return edges[0, LEV : LEV + 1]
        if r >= ROWS:
            return edges[1, LEV : LEV + 1]
        return t[r, LEV : LEV + 1, :]

    odd = lane % 2 == 1
    side = jnp.where(odd, west, east)

    def compact(far, own, towards):
        near = far
        number = near[LEV : LEV + 1, :]
        around = (
            pltpu.roll(near, 2, 1)
            + pltpu.roll(near, COLS - 2, 1)
            + pltpu.roll(near, towards, 1)
            + pltpu.roll(own[...], towards, 1)
        )
        return near + number * (around - 4.0 * near)

    side_next = jnp.where(odd, compact(west, mine_w, 1), compact(east, mine_e, COLS - 1))
    first_lane, last_lane = lane == 0, lane == COLS - 1

    def substep(above, here, below, number, sides, r):
        edge = pltpu.roll(sides, (-(2 * r + 3)) % COLS, 1)
        left = jnp.where(first_lane, edge, pltpu.roll(here, 1, 1))
        right = jnp.where(last_lane, edge, pltpu.roll(here, COLS - 1, 1))
        return here + number * (above + below + left + right - 4.0 * here)

    for r in range(-1, ROWS + 1):
        step_s[r + 1] = substep(state(r - 1), state(r), state(r + 1), number(r), side, r)
        if r >= 1:
            q = r - 1
            done = substep(step_s[q], step_s[q + 1], step_s[q + 2], number(q), side_next, q)
            temp_s[q] = done + heat[q]
            temp_out(q).start()
    for r in range(ROWS):
        heat_out(r).wait()
    for r in range(ROWS):
        temp_out(r).wait()


def diffuse(t, heat, gather_a, gather_b, mine_w, mine_e):
    whole = jax.ShapeDtypeStruct((LEV, ROWS, COLS), F32)
    return pl.pallas_call(
        diffuse_kernel,
        out_shape=(whole, whole),
        in_specs=[VMEM, VMEM, HBM, HBM, VMEM, VMEM],
        out_specs=(HBM, HBM),
        scratch_shapes=[
            pltpu.VMEM((2, 2 * PAD, COLS), F32),
            pltpu.VMEM((6, PAD, COLS), F32),
            pltpu.VMEM((ROWS + 2, PAD, COLS), F32),
            pltpu.VMEM((ROWS, PAD, COLS), F32),
            pltpu.SemaphoreType.DMA((3,)),
        ],
        compiler_params=pltpu.CompilerParams(vmem_limit_bytes=16 << 20),
        cost_estimate=pl.CostEstimate(flops=10**7, bytes_accessed=8 * 10**6, transcendentals=0),
    )(t, heat, *in_hbm(gather_a, gather_b), mine_w, mine_e)


def on_device(t, m, s, lit, k, w1, b1, w2, b2, w4, b4):
    lats, lons = lax.axis_size("lat"), lax.axis_size("lon")
    lit_row = jnp.concatenate([lit.reshape(1, ROWS), jnp.ones((1, COLS - ROWS), jnp.int32)], axis=1)
    t, pay_a, pay_b, west, east = pack(t, k)

    def group(first):
        pair = [first, (first + 1) % lons]
        return [lon * lats + lat for lon in pair for lat in range(lats)]

    gather_a = lax.all_gather(pay_a, ("lon", "lat"), axis_index_groups=[group(i) for i in range(0, lons, 2)])
    gather_b = lax.all_gather(pay_b, ("lon", "lat"), axis_index_groups=[group(i) for i in range(1, lons, 2)])
    heat = heat_of(lit_row, t, m, s, w1.T, b1.reshape(1, HID), w2, b2, w4, b4.reshape(1, LEV))
    return diffuse(t, heat, gather_a, gather_b, west, east)


def solution(mesh):
    whole, plane = P(None, "lat", "lon"), P("lat", "lon")
    return jax.shard_map(
        on_device,
        mesh=mesh,
        in_specs=(whole, whole, plane, plane, plane) + (P(),) * 6,
        out_specs=(whole, whole),
        check_vma=False,
    )
```

time: 37.8 us -> 103 us (2.72)
  the two profiles are of different devices: /device:TPU:8 before, /device:TPU:1 now
where the time goes in v3:
time: 103 us
  waiting for transfers between devices  77.6 us (75%)
  between operations  14.1 us (14%)
  Pallas kernels  11 us (11%)
    all_gather x1, waiting for transfers between devices, on_device(): lax.all_gather(pay_b, ('lon', 'lat'), axis_index_groups=[group(i) for i i...  39.5 us
    all_gather x1, waiting for transfers between devices, on_device(): lax.all_gather(pay_a, ('lon', 'lat'), axis_index_groups=[group(i) for i i...  37.4 us
    pallas_call x1, Pallas kernels, diffuse(): pl.pallas_call(diffuse_kernel, out_shape=(whole, whole), in_specs=[VMEM,...  4.97 us
    pallas_call x1, Pallas kernels, pack(): pl.pallas_call(pack_kernel, out_shape=(TRACK, jax.ShapeDtypeStruct((PAY_A...  3.18 us
    pallas_call x1, Pallas kernels, heat_of(): pl.pallas_call(heat_kernel, out_shape=TRACK, in_specs=[VMEM] * 2 + [HBM]...  2.84 us
  transfers between devices with their start and end apart: 2, of which 2 were waited for; matrix products, arithmetic and copies ran while one was open for 0% of the time, Pallas kernels for 3%

profile of v3, /device:TPU:1, one launch (start us, length us, event | category | flops | bytes accessed | tf_op | source)
XLA Modules:
  0.0 102.7 jit_solution(3081868249924335763)
XLA Ops:
  7.2 0.0 copy-start
  7.2 0.0 all-gather.7.cloned.1.call-start
  7.2 3.2 %shard_map.122 = (f32[32,96,128]{2,1,0:T(8,128)S(1)}, f32[480,128]{1,0:T(8,128)}, f32[256,128]{1,0:T(8,128)}, f32[96,128]{1,0:T(8,128)S(1)}, f32[96,128]{1,0:T(8,128)S(1)}) custom-call(f32[90,32,128]{2,1,0:T(8,128)} %t_hbm.1, f32[32,128]{1,0:T(8,128)} %k_hbm.1), custom_call_target="tpu_custom_call" | custom-call | flops 1000000 | bytes 4000000 | tf_op jit(solution)/shard_map/pallas_call | solution.py:138
  10.4 0.0 all-gather.7.cloned.1.call-update
  10.4 0.0 all-gather.5.cloned.1.call-start
  10.5 0.7 all-gather.5.cloned.1.call-update
  11.2 0.0 copy-done
  11.2 2.8 %shard_map.123.heat = f32[32,96,128]{2,1,0:T(8,128)S(1)} custom-call(s32[1,128]{1,0:T(1,128)S(1)} %concatenate.3.lit_row, f32[32,96,128]{2,1,0:T(8,128)S(1)} %get-tuple-element.7.t, f32[90,32,128]{2,1,0:T(8,128)} %m_hbm.1, f32[32,128]{1,0:T(8,128)} %s_hbm.1, f32[181,512]{1,0:T(8,128)} %bitcast.8, f32[1,512]{1,0:T(1,128)} %bitcast.9, f32[2,512,512]{2,1,0:T(8,128)} %w2_hbm.1, ...), custom_call_target="tpu_custom_call" | custom-call | flops 20000000000 | bytes 8000000 | tf_op jit(solution)/shard_map/pallas_call | solution.py:313
  14.1 39.5 %all-gather.7.cloned.1.call-done = f32[2048,128]{1,0:T(8,128)} async-done(((f32[256,128]{1,0:T(8,128)}), f32[2048,128]{1,0:T(8,128)}) %all-gather.7.cloned.1.call-update) | async-done | bytes 1048592 | tf_op jit(solution)/shard_map/all_gather | solution.py:461
  53.6 37.4 %all-gather.5.cloned.1.call-done = f32[3840,128]{1,0:T(8,128)} async-done(((f32[480,128]{1,0:T(8,128)}), f32[3840,128]{1,0:T(8,128)}) %all-gather.5.cloned.1.call-update) | async-done | bytes 1966096 | tf_op jit(solution)/shard_map/all_gather | solution.py:460
  90.9 5.0 %shard_map.124 = (f32[90,32,128]{2,1,0:T(8,128)}, f32[90,32,128]{2,1,0:T(8,128)}) custom-call(f32[32,96,128]{2,1,0:T(8,128)S(1)} %get-tuple-element.7.t, f32[32,96,128]{2,1,0:T(8,128)S(1)} %shard_map.123.heat, f32[8,480,128]{2,1,0:T(8,128)} %bitcast.6, f32[8,256,128]{2,1,0:T(8,128)} %bitcast.7, f32[96,128]{1,0:T(8,128)S(1)} %get-tuple-element.10.mine_w, ...), custom_call_target="tpu_custom_call" | custom-call | flops 10000000 | bytes 8000000 | tf_op jit(solution)/shard_map/pallas_call | solution.py:434
  (1 shorter events, 0.0 us)
Async XLA Ops:
  7.2 4.0 %copy-start = (s32[32,1]{0,1:T(1,128)S(1)}, s32[32,1]{0,1:T(1,128)}, u32[]{:S(2)}) copy-start(s32[32,1]{0,1:T(1,128)} %param.14) | copy-start | bytes 388
  7.2 46.4 %all-gather.7.cloned.1.call-start = ((), (), s32[]{:S(2)}) async-start(), calls=%async_computation.1 | async-start | bytes 1179648 | tf_op jit(solution)/shard_map/all_gather | solution.py:461
  10.4 80.5 %all-gather.5.cloned.1.call-start = ((), (), s32[]{:S(2)}) async-start(), calls=%async_computation | async-start | bytes 2211840 | tf_op jit(solution)/shard_map/all_gather | solution.py:460
Sparse Core Ops, SparseCore 0:
  10.6 42.9 all-gather.6
  56.0 34.8 all-gather.4

commit v4 on v2

--- a/solution.py
+++ b/solution.py
@@ -20,6 +20,7 @@
 KIN = 2 * PAD
 CHUNK = 8
 GROUPS = 4
+EARLY = 2
 W_LO = 2.0**15
 W_HI = 2.0**6
 X_LO = 2.0**9
@@ -301,34 +302,64 @@
     return [info[c * CHUNK + j] for j in range(CHUNK)]
 
 
-ROW_BLOCK = jax.ShapeDtypeStruct((CHUNK, PAD, COLS), F32)
-
-
-def some_rows_kernel(c, lit_row, t, m, w1s, w18, w2s, w28, w4s, bs, sc, out, lit_s, info, sem):
-    net = (t, m, w1s, w18, w2s, w28, w4s, bs, sc)
+def starts_early():
+    return lax.axis_index("lon") < EARLY
+
+
+def list_or_all(lit_row, lit_s, info, sem):
     every = all_lit(lit_row)
-
-    def put(j, row, value):
-        out[j] = value
 
     @pl.when(every)
     def _():
-        network_chunk(list(range(c * CHUNK, (c + 1) * CHUNK)), *net, put)
+        for r in range(ROWS):
+            info[r] = r
+        info[ROWS] = ROWS
 
     @pl.when(jnp.logical_not(every))
     def _():
-        n = count_lit(lit_row, lit_s, info, sem)
-
-        @pl.when(n > c * CHUNK)
-        def _():
-            network_chunk(listed(info, c), *net, put)
-
-
-def some_rows(c, *arrays):
+        count_lit(lit_row, lit_s, info, sem)
+
+    return info[ROWS]
+
+
+def before_kernel(lit_row, t, m, w1s, w18, w2s, w28, w4s, bs, sc, out, lit_s, info, sem):
+    n = list_or_all(lit_row, lit_s, info, sem)
+    chunks = jnp.minimum((n + CHUNK - 1) // CHUNK, jnp.where(starts_early(), 2, 1))
+
+    def one(c, _):
+        def put(j, row, value):
+            out[c * CHUNK + j] = value
+
+        network_chunk(listed(info, c), t, m, w1s, w18, w2s, w28, w4s, bs, sc, put)
+        return 0
+
+    lax.fori_loop(0, chunks, one, 0)
+
+
+def after_kernel(lit_row, before, t, m, w1s, w18, w2s, w28, w4s, bs, sc, out, lit_s, info, sem):
+    n = list_or_all(lit_row, lit_s, info, sem)
+    early = starts_early()
+
+    @pl.when(early)
+    def _():
+        out[0:CHUNK] = before[CHUNK : 2 * CHUNK]
+
+    def one(c, _):
+        def put(j, row, value):
+            out[(c - 1) * CHUNK + j] = value
+
+        network_chunk(listed(info, c), t, m, w1s, w18, w2s, w28, w4s, bs, sc, put)
+        return 0
+
+    start = jnp.where(early, 2, 1)
+    lax.fori_loop(start, jnp.minimum((n + CHUNK - 1) // CHUNK, 2 * start), one, 0)
+
+
+def some_rows(kernel, blocks, *arrays):
     return pl.pallas_call(
-        functools.partial(some_rows_kernel, c),
-        out_shape=ROW_BLOCK,
-        in_specs=[VMEM] * 10,
+        kernel,
+        out_shape=jax.ShapeDtypeStruct((blocks * CHUNK, PAD, COLS), F32),
+        in_specs=[VMEM] * len(arrays),
         out_specs=VMEM,
         scratch_shapes=LIST_SCRATCH,
         compiler_params=pltpu.CompilerParams(vmem_limit_bytes=32 << 20),
@@ -341,7 +372,8 @@
     heat_hbm, temp_hbm, lit_s, info, list_sem, heat_s, step_s, temp_s, sems,
 ):
     net = (t, m, w1s, w18, w2s, w28, w4s, bs, sc)
-    every = all_lit(lit_row)
+    early = starts_early()
+    fused = jnp.logical_and(all_lit(lit_row), jnp.logical_not(early))
 
     def heat_out(r, src=None, at=None):
         src, at = (heat_s, r) if src is None else (src, at)
@@ -399,7 +431,7 @@
         temp_s[r] = done + heat
         temp_out(r).start()
 
-    @pl.when(every)
+    @pl.when(fused)
     def _():
         blocks = (heat_a, heat_b)
         early = [heat_out(r, blocks[r // CHUNK], r % CHUNK) for r in range(2 * CHUNK)]
@@ -436,21 +468,27 @@
         for r in range(ROWS):
             temp_out(r).wait()
 
-    @pl.when(jnp.logical_not(every))
+    @pl.when(jnp.logical_not(fused))
     def _():
-        n = count_lit(lit_row, lit_s, info, list_sem)
-        heat_s[...] = jnp.zeros_like(heat_s)
-        for part, block in ((0, heat_a), (1, heat_b)):
-            @pl.when(n > part * CHUNK)
+        n = list_or_all(lit_row, lit_s, info, list_sem)
+        chunks = (n + CHUNK - 1) // CHUNK
+
+        @pl.when(n < ROWS)
+        def _():
+            heat_s[...] = jnp.zeros_like(heat_s)
+
+        for part in range(ROWS // CHUNK):
+            @pl.when(jnp.logical_and(part < chunks, jnp.logical_or(early, part < 2)))
             def _():
                 for j in range(CHUNK):
-                    heat_s[info[part * CHUNK + j]] = block[j]
+                    block = heat_a[j] if part == 0 else heat_b[(part - 1) * CHUNK + j]
+                    heat_s[info[part * CHUNK + j]] = block
 
         def one(c, _):
             network_chunk(listed(info, c), *net, put)
             return 0
 
-        lax.fori_loop(2, (n + CHUNK - 1) // CHUNK, one, 0)
+        lax.fori_loop(jnp.where(early, chunks, 2), chunks, one, 0)
         for r in range(ROWS):
             heat_out(r).start()
         for r in range(-1, ROWS + 1):
@@ -491,11 +529,11 @@
     )
     north = lax.ppermute(down, "lat", [(i, i + 1) for i in range(lats - 1)])
     south = lax.ppermute(up, "lat", [(i + 1, i) for i in range(lats - 1)])
-    heat_a = some_rows(0, lit_row, t, m, *net)
+    heat_a = some_rows(before_kernel, 2, lit_row, t, m, *net)
     west, east = corners(north, south, west, east)
     from_east = lax.ppermute(west, "lon", [(i, (i - 1) % lons) for i in range(lons)])
     from_west = lax.ppermute(east, "lon", [(i, (i + 1) % lons) for i in range(lons)])
-    heat_b = some_rows(1, lit_row, t, m, *net)
+    heat_b = some_rows(after_kernel, 3, lit_row, heat_a, t, m, *net)
     return last(lit_row, t, m, *net, heat_a, heat_b, north, south, west, east, from_west, from_east)
 
 

time: 37.8 us -> 33 us (0.87)
  starting transfers between devices: 12.5 us -> 7.68 us
  Pallas kernels: 21 us -> 18.4 us
  waiting for transfers between devices: 3.31 us -> 5.62 us
    ppermute x1, starting transfers between devices: 6.64 us -> 1.83 us  [on_device(): lax.ppermute(west, 'lon', [(i, (i - 1) % lons) for i in range(lons)])]
    pallas_call x1, Pallas kernels: 9.49 us -> 4.96 us  [last(): pl.pallas_call(last_kernel, out_shape=(whole, whole), in_specs=[VMEM] * 1...]
    ppermute x1, waiting for transfers between devices: 2.92 us -> 5.08 us  [on_device(): lax.ppermute(east, 'lon', [(i, (i + 1) % lons) for i in range(lons)])]
    pallas_call x2, Pallas kernels: 7.61 us -> 9.6 us  [some_rows(): pl.pallas_call(kernel, out_shape=jax.ShapeDtypeStruct((blocks * CHUNK, PA...]
    ppermute x1, waiting for transfers between devices: 0.01 us -> 0.53 us  [on_device(): lax.ppermute(west, 'lon', [(i, (i - 1) % lons) for i in range(lons)])]
    ppermute x1, waiting for transfers between devices: 0.38 us -> 0.01 us  [on_device(): south = lax.ppermute(up, 'lat', [(i + 1, i) for i in range(lats - 1)])]
  transfers between devices with their start and end apart: 4 -> 4, of which waited for: 2 -> 2; matrix products, arithmetic and copies ran while one was open for 0% -> 0% of each run, Pallas kernels for 20% -> 29%
where the time goes in v4:
time: 33 us; the launch traced here: 32.6 us
  Pallas kernels  18.4 us (56%)
  starting transfers between devices  7.68 us (23%)
  waiting for transfers between devices  5.62 us (17%)
  between operations  0.88 us (3%)
    pallas_call x2, Pallas kernels, some_rows(): pl.pallas_call(kernel, out_shape=jax.ShapeDtypeStruct((blocks * CHUNK, PA...  9.6 us
    ppermute x1, waiting for transfers between devices, on_device(): lax.ppermute(east, 'lon', [(i, (i + 1) % lons) for i in range(lons)])  5.08 us
    pallas_call x1, Pallas kernels, last(): pl.pallas_call(last_kernel, out_shape=(whole, whole), in_specs=[VMEM] * 1...  4.96 us
    pallas_call x1, Pallas kernels, load(): pl.pallas_call(load_kernel, out_shape=(TRACK, TRACK) + tuple((jax.ShapeDt...  3.75 us
    ppermute x1, starting transfers between devices, on_device(): north = lax.ppermute(down, 'lat', [(i, i + 1) for i in range(lats - 1)])  3.48 us
    ppermute x1, starting transfers between devices, on_device(): south = lax.ppermute(up, 'lat', [(i + 1, i) for i in range(lats - 1)])  2.36 us
    ppermute x1, starting transfers between devices, on_device(): lax.ppermute(west, 'lon', [(i, (i - 1) % lons) for i in range(lons)])  1.83 us
  transfers between devices with their start and end apart: 4, of which 2 were waited for; matrix products, arithmetic and copies ran while one was open for 0% of the time, Pallas kernels for 29%

profile of v4, /device:TPU:8, one launch (start us, length us, event | category | flops | bytes accessed | tf_op | source)
XLA Modules:
  0.0 32.6 jit_solution(11428815333614055012)
XLA Ops:
  0.6 0.0 copy-start
  0.6 3.8 %shard_map.122 = (f32[32,96,128]{2,1,0:T(8,128)S(1)}, f32[32,96,128]{2,1,0:T(8,128)S(1)}, bf16[512,192]{1,0:T(8,128)(2,1)S(1)}, f8e4m3fn[512,384]{1,0:T(32,128)(...) custom-call(f32[90,32,128]{2,1,0:T(8,128)} %t_hbm.1, ...), custom_call_target="tpu_custom_call" | custom-call | flops 1000000 | bytes 8000000 | tf_op jit(solution)/shard_map/pallas_call | solution.py:164
  4.4 3.5 %collective-permute-start = (f32[192,128]{1,0:T(8,128)S(1)}, f32[192,128]{1,0:T(8,128)S(1)}, u32[]{:S(2)}, u32[]{:S(2)}) collective-permute-start(f32[192,128]{1,0:T(8,128)S(1)} %get-tuple-element.26), channel_id=1, source_target_pairs={{0,1},{1,2},{2,3},{4,5},{5,6},{6,7},{8,9},{9,10},{10,11},{12,13},{... | collective-permute-start | bytes 294920 | tf_op jit(solution)/shard_map/ppermute | solution.py:530
  7.9 2.4 %collective-permute-start.1 = (f32[192,128]{1,0:T(8,128)S(1)}, f32[192,128]{1,0:T(8,128)S(1)}, u32[]{:S(2)}, u32[]{:S(2)}) collective-permute-start(f32[192,128]{1,0:T(8,128)S(1)} %get-tuple-element.27), channel_id=1, source_target_pairs={{1,0},{2,1},{3,2},{5,4},{6,5},{7,6},{9,8},{10,9},{11,10},{13,12},{... | collective-permute-start | bytes 294920 | tf_op jit(solution)/shard_map/ppermute | solution.py:531
  10.3 0.0 copy-done
  10.3 8.4 %shard_map.123.before.heat_a = f32[16,96,128]{2,1,0:T(8,128)S(1)} custom-call(s32[1,128]{1,0:T(1,128)S(1)} %concatenate.3.lit_row, f32[32,96,128]{2,1,0:T(8,128)S(1)} %get-tuple-element.17.t, f32[32,96,128]{2,1,0:T(8,128)S(1)} %get-tuple-element.18.m, bf16[512,192]{1,0:T(8,128)(2,1)S(1)} %get-tuple-element.19.w1s, ...), custom_call_target="tpu_custom_call" | custom-call | flops 5000000000 | bytes 8000000 | tf_op jit(solution)/shard_map/pallas_call | solution.py:359
  18.7 0.0 collective-permute-done.north_ref.north
  18.7 0.0 collective-permute-done.1.south_ref.south
  18.7 0.1 shard_map.125
  18.8 1.8 %collective-permute-start.3 = (f32[96,128]{1,0:T(8,128)S(1)}, f32[96,128]{1,0:T(8,128)S(1)}, u32[]{:S(2)}, u32[]{:S(2)}) collective-permute-start(f32[96,128]{1,0:T(8,128)S(1)} %get-tuple-element.30.mine_w), channel_id=1, source_target_pairs={{0,252},{4,0},{8,4},{12,8},{16,12},{20,16},{24,20},{28,24},{32,28}... | collective-permute-start | bytes 147464 | tf_op jit(solution)/shard_map/ppermute | solution.py:534
  20.7 0.0 collective-permute-start.2
  20.7 1.2 %shard_map.124.heat_b = f32[24,96,128]{2,1,0:T(8,128)S(1)} custom-call(s32[1,128]{1,0:T(1,128)S(1)} %concatenate.3.lit_row, f32[16,96,128]{2,1,0:T(8,128)S(1)} %shard_map.123.before.heat_a, f32[32,96,128]{2,1,0:T(8,128)S(1)} %get-tuple-element.17.t, f32[32,96,128]{2,1,0:T(8,128)S(1)} %get-tuple-element.18.m, bf16[512,192]{1,0:T(8,128)(2,1)S(1)} %get-tuple-element.19.w1s, ...), custom_call_target="tpu_custom_call" | custom-call | flops 5000000000 | bytes 8000000 | tf_op jit(solution)/shard_map/pallas_call | solution.py:359
  21.9 0.5 %collective-permute-done.3.east = f32[96,128]{1,0:T(8,128)S(1)} collective-permute-done((f32[96,128]{1,0:T(8,128)S(1)}, f32[96,128]{1,0:T(8,128)S(1)}, u32[]{:S(2)}, u32[]{:S(2)}) %collective-permute-start.3) | collective-permute-done | bytes 49184 | tf_op jit(solution)/shard_map/ppermute | solution.py:534
  22.4 5.1 %collective-permute-done.2.west = f32[96,128]{1,0:T(8,128)S(1)} collective-permute-done((f32[96,128]{1,0:T(8,128)S(1)}, f32[96,128]{1,0:T(8,128)S(1)}, u32[]{:S(2)}, u32[]{:S(2)}) %collective-permute-start.2) | collective-permute-done | bytes 49184 | tf_op jit(solution)/shard_map/ppermute | solution.py:535
  27.5 5.0 %shard_map.126 = (f32[90,32,128]{2,1,0:T(8,128)}, f32[90,32,128]{2,1,0:T(8,128)}) custom-call(s32[1,128]{1,0:T(1,128)S(1)} %concatenate.3.lit_row, f32[32,96,128]{2,1,0:T(8,128)S(1)} %get-tuple-element.17.t, f32[32,96,128]{2,1,0:T(8,128)S(1)} %get-tuple-element.18.m, bf16[512,192]{1,0:T(8,128)(2,1)S(1)} %get-tuple-element.19.w1s, ...), custom_call_target="tpu_custom_call" | custom-call | flops 10000000000 | bytes 8000000 | tf_op jit(solution)/shard_map/pallas_call | solution.py:507
  (1 shorter events, 0.0 us)
Async XLA Ops:
  0.6 9.6 %copy-start = (s32[32,1]{0,1:T(1,128)S(1)}, s32[32,1]{0,1:T(1,128)}, u32[]{:S(2)}) copy-start(s32[32,1]{0,1:T(1,128)} %param.14) | copy-start | bytes 388
  4.4 14.3 %collective-permute-start = (f32[192,128]{1,0:T(8,128)S(1)}, f32[192,128]{1,0:T(8,128)S(1)}, u32[]{:S(2)}, u32[]{:S(2)}) collective-permute-start(f32[192,128]{1,0:T(8,128)S(1)} %get-tuple-element.26), channel_id=1, source_target_pairs={{0,1},{1,2},{2,3},{4,5},{5,6},{6,7},{8,9},{9,10},{10,11},{12,13},{... | collective-permute-start | bytes 294920 | tf_op jit(solution)/shard_map/ppermute | solution.py:530
  7.9 10.8 %collective-permute-start.1 = (f32[192,128]{1,0:T(8,128)S(1)}, f32[192,128]{1,0:T(8,128)S(1)}, u32[]{:S(2)}, u32[]{:S(2)}) collective-permute-start(f32[192,128]{1,0:T(8,128)S(1)} %get-tuple-element.27), channel_id=1, source_target_pairs={{1,0},{2,1},{3,2},{5,4},{6,5},{7,6},{9,8},{10,9},{11,10},{13,12},{... | collective-permute-start | bytes 294920 | tf_op jit(solution)/shard_map/ppermute | solution.py:531
  18.8 3.6 %collective-permute-start.3 = (f32[96,128]{1,0:T(8,128)S(1)}, f32[96,128]{1,0:T(8,128)S(1)}, u32[]{:S(2)}, u32[]{:S(2)}) collective-permute-start(f32[96,128]{1,0:T(8,128)S(1)} %get-tuple-element.30.mine_w), channel_id=1, source_target_pairs={{0,252},{4,0},{8,4},{12,8},{16,12},{20,16},{24,20},{28,24},{32,28}... | collective-permute-start | bytes 147464 | tf_op jit(solution)/shard_map/ppermute | solution.py:534
  20.7 6.8 %collective-permute-start.2 = (f32[96,128]{1,0:T(8,128)S(1)}, f32[96,128]{1,0:T(8,128)S(1)}, u32[]{:S(2)}, u32[]{:S(2)}) collective-permute-start(f32[96,128]{1,0:T(8,128)S(1)} %get-tuple-element.31.mine_e), channel_id=1, source_target_pairs={{0,4},{4,8},{8,12},{12,16},{16,20},{20,24},{24,28},{28,32},{32,36}... | collective-permute-start | bytes 147464 | tf_op jit(solution)/shard_map/ppermute | solution.py:535

commit v5 on v4

--- a/solution.py
+++ b/solution.py
@@ -352,7 +352,7 @@
         return 0
 
     start = jnp.where(early, 2, 1)
-    lax.fori_loop(start, jnp.minimum((n + CHUNK - 1) // CHUNK, 2 * start), one, 0)
+    lax.fori_loop(start, jnp.minimum((n + CHUNK - 1) // CHUNK, start + 2), one, 0)
 
 
 def some_rows(kernel, blocks, *arrays):
@@ -433,37 +433,38 @@
 
     @pl.when(fused)
     def _():
-        blocks = (heat_a, heat_b)
-        early = [heat_out(r, blocks[r // CHUNK], r % CHUNK) for r in range(2 * CHUNK)]
-        for copy in early:
+        def known(r):
+            return (heat_a, r) if r < CHUNK else (heat_b, r - CHUNK)
+
+        copies = [heat_out(r, *known(r)) for r in range(3 * CHUNK)]
+        for copy in copies:
             copy.start()
-        ahead = iter(range(-1, ROWS + 1))
-
-        def between_one():
-            for r in (next(ahead, None), next(ahead, None), next(ahead, None)):
-                if r is not None:
-                    step_one(r)
-
-        rows = list(range(2 * CHUNK, 3 * CHUNK))
-        network_chunk(rows, *net, put, between_one)
-        late = [heat_out(r) for r in rows]
-        for copy in late:
-            copy.start()
-        behind = iter(range(3 * CHUNK))
-
-        def between_two():
-            for r in (next(behind, None), next(behind, None)):
-                if r is not None:
-                    step_two(r, blocks[r // CHUNK][r % CHUNK] if r < 2 * CHUNK else heat_s[r])
+
+        def tasks():
+            for r in range(-1, ROWS + 1):
+                step_one(r)
+                yield
+                if 1 <= r <= 3 * CHUNK:
+                    block, at = known(r - 1)
+                    step_two(r - 1, block[at])
+                    yield
+
+        todo = tasks()
+
+        def between():
+            for _ in range(4):
+                next(todo, None)
 
         rows = list(range(3 * CHUNK, ROWS))
-        network_chunk(rows, *net, put, between_two)
+        network_chunk(rows, *net, put, between)
+        for _ in todo:
+            pass
         for r in rows:
             copy = heat_out(r)
             copy.start()
-            late.append(copy)
+            copies.append(copy)
             step_two(r, heat_s[r])
-        for copy in early + late:
+        for copy in copies:
             copy.wait()
         for r in range(ROWS):
             temp_out(r).wait()
@@ -478,7 +479,7 @@
             heat_s[...] = jnp.zeros_like(heat_s)
 
         for part in range(ROWS // CHUNK):
-            @pl.when(jnp.logical_and(part < chunks, jnp.logical_or(early, part < 2)))
+            @pl.when(jnp.logical_and(part < chunks, jnp.logical_or(early, part < 3)))
             def _():
                 for j in range(CHUNK):
                     block = heat_a[j] if part == 0 else heat_b[(part - 1) * CHUNK + j]
@@ -488,7 +489,7 @@
             network_chunk(listed(info, c), *net, put)
             return 0
 
-        lax.fori_loop(jnp.where(early, chunks, 2), chunks, one, 0)
+        lax.fori_loop(jnp.where(early, chunks, 3), chunks, one, 0)
         for r in range(ROWS):
             heat_out(r).start()
         for r in range(-1, ROWS + 1):

time: 33 us -> 32.8 us (level)
  waiting for transfers between devices: 5.62 us -> 0.01 us
  Pallas kernels: 18.4 us -> 22.5 us
  starting transfers between devices: 7.68 us -> 9.25 us
    pallas_call x2, Pallas kernels: 9.6 us -> 14.7 us  [some_rows(): pl.pallas_call(kernel, out_shape=jax.ShapeDtypeStruct((blocks * CHUNK, PA...]
    ppermute x1, waiting for transfers between devices: 5.08 us -> 0.01 us  [on_device(): lax.ppermute(east, 'lon', [(i, (i + 1) % lons) for i in range(lons)])]
    ppermute x1, starting transfers between devices: 1.83 us -> 3.41 us  [on_device(): lax.ppermute(west, 'lon', [(i, (i - 1) % lons) for i in range(lons)])]
    pallas_call x1, Pallas kernels: 4.96 us -> 3.91 us  [last(): pl.pallas_call(last_kernel, out_shape=(whole, whole), in_specs=[VMEM] * 1...]
    ppermute x1, waiting for transfers between devices: 0.53 us -> 0.01 us  [on_device(): lax.ppermute(west, 'lon', [(i, (i - 1) % lons) for i in range(lons)])]
  transfers between devices with their start and end apart: 4 -> 4, of which waited for: 2 -> 0; matrix products, arithmetic and copies ran while one was open for 0% -> 0% of each run, Pallas kernels for 29% -> 45%
where the time goes in v5:
time: 32.8 us; the launch traced here: 32.7 us
  Pallas kernels  22.5 us (69%)
  starting transfers between devices  9.25 us (28%)
  between operations  0.9 us (3%)
    pallas_call x2, Pallas kernels, some_rows(): pl.pallas_call(kernel, out_shape=jax.ShapeDtypeStruct((blocks * CHUNK, PA...  14.7 us
    pallas_call x1, Pallas kernels, last(): pl.pallas_call(last_kernel, out_shape=(whole, whole), in_specs=[VMEM] * 1...  3.91 us
    pallas_call x1, Pallas kernels, load(): pl.pallas_call(load_kernel, out_shape=(TRACK, TRACK) + tuple((jax.ShapeDt...  3.75 us
    ppermute x1, starting transfers between devices, on_device(): north = lax.ppermute(down, 'lat', [(i, i + 1) for i in range(lats - 1)])  3.48 us
    ppermute x1, starting transfers between devices, on_device(): lax.ppermute(west, 'lon', [(i, (i - 1) % lons) for i in range(lons)])  3.41 us
    ppermute x1, starting transfers between devices, on_device(): south = lax.ppermute(up, 'lat', [(i + 1, i) for i in range(lats - 1)])  2.36 us
  transfers between devices with their start and end apart: 4, of which 0 were waited for; matrix products, arithmetic and copies ran while one was open for 0% of the time, Pallas kernels for 45%

profile of v5, /device:TPU:8, one launch (start us, length us, event | category | flops | bytes accessed | tf_op | source)
XLA Modules:
  0.0 32.7 jit_solution(16849807000913329830)
XLA Ops:
  0.6 0.0 copy-start
  0.6 3.8 %shard_map.122 = (f32[32,96,128]{2,1,0:T(8,128)S(1)}, f32[32,96,128]{2,1,0:T(8,128)S(1)}, bf16[512,192]{1,0:T(8,128)(2,1)S(1)}, f8e4m3fn[512,384]{1,0:T(32,128)(...) custom-call(f32[90,32,128]{2,1,0:T(8,128)} %t_hbm.1, ...), custom_call_target="tpu_custom_call" | custom-call | flops 1000000 | bytes 8000000 | tf_op jit(solution)/shard_map/pallas_call | solution.py:164
  4.4 3.5 %collective-permute-start = (f32[192,128]{1,0:T(8,128)S(1)}, f32[192,128]{1,0:T(8,128)S(1)}, u32[]{:S(2)}, u32[]{:S(2)}) collective-permute-start(f32[192,128]{1,0:T(8,128)S(1)} %get-tuple-element.26), channel_id=1, source_target_pairs={{0,1},{1,2},{2,3},{4,5},{5,6},{6,7},{8,9},{9,10},{10,11},{12,13},{... | collective-permute-start | bytes 294920 | tf_op jit(solution)/shard_map/ppermute | solution.py:531
  7.9 2.4 %collective-permute-start.1 = (f32[192,128]{1,0:T(8,128)S(1)}, f32[192,128]{1,0:T(8,128)S(1)}, u32[]{:S(2)}, u32[]{:S(2)}) collective-permute-start(f32[192,128]{1,0:T(8,128)S(1)} %get-tuple-element.27), channel_id=1, source_target_pairs={{1,0},{2,1},{3,2},{5,4},{6,5},{7,6},{9,8},{10,9},{11,10},{13,12},{... | collective-permute-start | bytes 294920 | tf_op jit(solution)/shard_map/ppermute | solution.py:532
  10.3 0.0 copy-done
  10.3 7.4 %shard_map.123.before.heat_a = f32[16,96,128]{2,1,0:T(8,128)S(1)} custom-call(s32[1,128]{1,0:T(1,128)S(1)} %concatenate.3.lit_row, f32[32,96,128]{2,1,0:T(8,128)S(1)} %get-tuple-element.17.t, f32[32,96,128]{2,1,0:T(8,128)S(1)} %get-tuple-element.18.m, bf16[512,192]{1,0:T(8,128)(2,1)S(1)} %get-tuple-element.19.w1s, ...), custom_call_target="tpu_custom_call" | custom-call | flops 5000000000 | bytes 8000000 | tf_op jit(solution)/shard_map/pallas_call | solution.py:359
  17.7 0.0 collective-permute-done.north_ref.north
  17.7 0.0 collective-permute-done.1.south_ref.south
  17.7 0.1 shard_map.125
  17.8 3.4 %collective-permute-start.3 = (f32[96,128]{1,0:T(8,128)S(1)}, f32[96,128]{1,0:T(8,128)S(1)}, u32[]{:S(2)}, u32[]{:S(2)}) collective-permute-start(f32[96,128]{1,0:T(8,128)S(1)} %get-tuple-element.30.mine_w), channel_id=1, source_target_pairs={{0,252},{4,0},{8,4},{12,8},{16,12},{20,16},{24,20},{28,24},{32,28}... | collective-permute-start | bytes 147464 | tf_op jit(solution)/shard_map/ppermute | solution.py:535
  21.2 0.0 collective-permute-start.2
  21.2 7.4 %shard_map.124.heat_b = f32[24,96,128]{2,1,0:T(8,128)S(1)} custom-call(s32[1,128]{1,0:T(1,128)S(1)} %concatenate.3.lit_row, f32[16,96,128]{2,1,0:T(8,128)S(1)} %shard_map.123.before.heat_a, f32[32,96,128]{2,1,0:T(8,128)S(1)} %get-tuple-element.17.t, f32[32,96,128]{2,1,0:T(8,128)S(1)} %get-tuple-element.18.m, bf16[512,192]{1,0:T(8,128)(2,1)S(1)} %get-tuple-element.19.w1s, ...), custom_call_target="tpu_custom_call" | custom-call | flops 5000000000 | bytes 8000000 | tf_op jit(solution)/shard_map/pallas_call | solution.py:359
  28.6 0.0 collective-permute-done.3.east
  28.6 0.0 collective-permute-done.2.west
  28.6 3.9 %shard_map.126 = (f32[90,32,128]{2,1,0:T(8,128)}, f32[90,32,128]{2,1,0:T(8,128)}) custom-call(s32[1,128]{1,0:T(1,128)S(1)} %concatenate.3.lit_row, f32[32,96,128]{2,1,0:T(8,128)S(1)} %get-tuple-element.17.t, f32[32,96,128]{2,1,0:T(8,128)S(1)} %get-tuple-element.18.m, bf16[512,192]{1,0:T(8,128)(2,1)S(1)} %get-tuple-element.19.w1s, ...), custom_call_target="tpu_custom_call" | custom-call | flops 10000000000 | bytes 8000000 | tf_op jit(solution)/shard_map/pallas_call | solution.py:508
  (1 shorter events, 0.0 us)
Async XLA Ops:
  0.6 9.6 %copy-start = (s32[32,1]{0,1:T(1,128)S(1)}, s32[32,1]{0,1:T(1,128)}, u32[]{:S(2)}) copy-start(s32[32,1]{0,1:T(1,128)} %param.14) | copy-start | bytes 388
  4.4 13.3 %collective-permute-start = (f32[192,128]{1,0:T(8,128)S(1)}, f32[192,128]{1,0:T(8,128)S(1)}, u32[]{:S(2)}, u32[]{:S(2)}) collective-permute-start(f32[192,128]{1,0:T(8,128)S(1)} %get-tuple-element.26), channel_id=1, source_target_pairs={{0,1},{1,2},{2,3},{4,5},{5,6},{6,7},{8,9},{9,10},{10,11},{12,13},{... | collective-permute-start | bytes 294920 | tf_op jit(solution)/shard_map/ppermute | solution.py:531
  7.9 9.8 %collective-permute-start.1 = (f32[192,128]{1,0:T(8,128)S(1)}, f32[192,128]{1,0:T(8,128)S(1)}, u32[]{:S(2)}, u32[]{:S(2)}) collective-permute-start(f32[192,128]{1,0:T(8,128)S(1)} %get-tuple-element.27), channel_id=1, source_target_pairs={{1,0},{2,1},{3,2},{5,4},{6,5},{7,6},{9,8},{10,9},{11,10},{13,12},{... | collective-permute-start | bytes 294920 | tf_op jit(solution)/shard_map/ppermute | solution.py:532
  17.8 10.8 %collective-permute-start.3 = (f32[96,128]{1,0:T(8,128)S(1)}, f32[96,128]{1,0:T(8,128)S(1)}, u32[]{:S(2)}, u32[]{:S(2)}) collective-permute-start(f32[96,128]{1,0:T(8,128)S(1)} %get-tuple-element.30.mine_w), channel_id=1, source_target_pairs={{0,252},{4,0},{8,4},{12,8},{16,12},{20,16},{24,20},{28,24},{32,28}... | collective-permute-start | bytes 147464 | tf_op jit(solution)/shard_map/ppermute | solution.py:535
  21.2 7.4 %collective-permute-start.2 = (f32[96,128]{1,0:T(8,128)S(1)}, f32[96,128]{1,0:T(8,128)S(1)}, u32[]{:S(2)}, u32[]{:S(2)}) collective-permute-start(f32[96,128]{1,0:T(8,128)S(1)} %get-tuple-element.31.mine_e), channel_id=1, source_target_pairs={{0,4},{4,8},{8,12},{12,16},{16,20},{20,24},{24,28},{28,32},{32,36}... | collective-permute-start | bytes 147464 | tf_op jit(solution)/shard_map/ppermute | solution.py:536

commit v6 on v5

--- a/solution.py
+++ b/solution.py
@@ -122,13 +122,17 @@
     for copy in state:
         copy.wait()
     blank = jnp.zeros((PAD - LEV - 1, COLS), F32)
+    lane = lane_index()
     west = jnp.zeros((PAD, COLS), F32)
     east = jnp.zeros((PAD, COLS), F32)
     for r in range(ROWS):
         t[r, LEV:PAD, :] = jnp.concatenate([k[r : r + 1, :], blank], axis=0)
-        west, east = first_columns(t[r], r, west, east)
+        place = 2 * (r + 1)
+        rolled = pltpu.roll(t[r], place, 1)
+        west = jnp.where((lane == place) | (lane == place + 1), rolled, west)
+        east = jnp.where((lane == place - 2) | (lane == place - 1), rolled, east)
     west_out[...] = west
-    east_out[...] = east
+    east_out[...] = pltpu.roll(east, 2, 1)
     up[0:PAD] = t[0]
     up[PAD:] = t[1]
     down[0:PAD] = t[ROWS - 1]
@@ -373,7 +377,7 @@
 ):
     net = (t, m, w1s, w18, w2s, w28, w4s, bs, sc)
     early = starts_early()
-    fused = jnp.logical_and(all_lit(lit_row), jnp.logical_not(early))
+    every = all_lit(lit_row)
 
     def heat_out(r, src=None, at=None):
         src, at = (heat_s, r) if src is None else (src, at)
@@ -431,25 +435,36 @@
         temp_s[r] = done + heat
         temp_out(r).start()
 
-    @pl.when(fused)
+    def known(r):
+        return (heat_a, r) if r < CHUNK else (heat_b, r - CHUNK)
+
+    def tasks(count):
+        for r in range(-1, ROWS + 1):
+            step_one(r)
+            yield
+            if 1 <= r <= count:
+                block, at = known(r - 1)
+                step_two(r - 1, block[at])
+                yield
+
+    @pl.when(jnp.logical_and(every, early))
     def _():
-        def known(r):
-            return (heat_a, r) if r < CHUNK else (heat_b, r - CHUNK)
-
+        copies = [heat_out(r, *known(r)) for r in range(ROWS)]
+        for copy in copies:
+            copy.start()
+        for _ in tasks(ROWS):
+            pass
+        for copy in copies:
+            copy.wait()
+        for r in range(ROWS):
+            temp_out(r).wait()
+
+    @pl.when(jnp.logical_and(every, jnp.logical_not(early)))
+    def _():
         copies = [heat_out(r, *known(r)) for r in range(3 * CHUNK)]
         for copy in copies:
             copy.start()
-
-        def tasks():
-            for r in range(-1, ROWS + 1):
-                step_one(r)
-                yield
-                if 1 <= r <= 3 * CHUNK:
-                    block, at = known(r - 1)
-                    step_two(r - 1, block[at])
-                    yield
-
-        todo = tasks()
+        todo = tasks(3 * CHUNK)
 
         def between():
             for _ in range(4):
@@ -469,15 +484,12 @@
         for r in range(ROWS):
             temp_out(r).wait()
 
-    @pl.when(jnp.logical_not(fused))
+    @pl.when(jnp.logical_not(every))
     def _():
-        n = list_or_all(lit_row, lit_s, info, list_sem)
+        n = count_lit(lit_row, lit_s, info, list_sem)
         chunks = (n + CHUNK - 1) // CHUNK
 
-        @pl.when(n < ROWS)
-        def _():
-            heat_s[...] = jnp.zeros_like(heat_s)
-
+        heat_s[...] = jnp.zeros_like(heat_s)
         for part in range(ROWS // CHUNK):
             @pl.when(jnp.logical_and(part < chunks, jnp.logical_or(early, part < 3)))
             def _():

time: 32.8 us -> 32.2 us (0.982)
  Pallas kernels: 22.5 us -> 10.8 us
  waiting for transfers between devices: 0.01 us -> 8.42 us
  starting transfers between devices: 9.25 us -> 12 us
    pallas_call x2, Pallas kernels: 14.7 us -> 2.51 us  [some_rows(): pl.pallas_call(kernel, out_shape=jax.ShapeDtypeStruct((blocks * CHUNK, PA...]
    ppermute x1, waiting for transfers between devices: 0.01 us -> 5.08 us  [on_device(): lax.ppermute(east, 'lon', [(i, (i + 1) % lons) for i in range(lons)])]
    ppermute x1, waiting for transfers between devices: 0.01 us -> 2.86 us  [on_device(): south = lax.ppermute(up, 'lat', [(i + 1, i) for i in range(lats - 1)])]
    ppermute x1, starting transfers between devices: 3.41 us -> 6.14 us  [on_device(): lax.ppermute(west, 'lon', [(i, (i - 1) % lons) for i in range(lons)])]
    pallas_call x1, Pallas kernels: 3.91 us -> 4.83 us  [last(): pl.pallas_call(last_kernel, out_shape=(whole, whole), in_specs=[VMEM] * 1...]
    ppermute x1, waiting for transfers between devices: 0.01 us -> 0.47 us  [on_device(): lax.ppermute(west, 'lon', [(i, (i - 1) % lons) for i in range(lons)])]
    pallas_call x1, Pallas kernels: 3.75 us -> 3.39 us  [load(): pl.pallas_call(load_kernel, out_shape=(TRACK, TRACK) + tuple((jax.ShapeDt...]
  transfers between devices with their start and end apart: 4 -> 4, of which waited for: 0 -> 3; matrix products, arithmetic and copies ran while one was open for 0% -> 0% of each run, Pallas kernels for 45% -> 8%
where the time goes in v6:
time: 32.2 us; the launch traced here: 32.1 us
  starting transfers between devices  12 us (37%)
  Pallas kernels  10.8 us (34%)
  waiting for transfers between devices  8.42 us (26%)
  between operations  0.87 us (3%)
    ppermute x1, starting transfers between devices, on_device(): lax.ppermute(west, 'lon', [(i, (i - 1) % lons) for i in range(lons)])  6.14 us
    ppermute x1, waiting for transfers between devices, on_device(): lax.ppermute(east, 'lon', [(i, (i + 1) % lons) for i in range(lons)])  5.08 us
    pallas_call x1, Pallas kernels, last(): pl.pallas_call(last_kernel, out_shape=(whole, whole), in_specs=[VMEM] * 1...  4.83 us
    ppermute x1, starting transfers between devices, on_device(): north = lax.ppermute(down, 'lat', [(i, i + 1) for i in range(lats - 1)])  3.48 us
    pallas_call x1, Pallas kernels, load(): pl.pallas_call(load_kernel, out_shape=(TRACK, TRACK) + tuple((jax.ShapeDt...  3.39 us
    ppermute x1, waiting for transfers between devices, on_device(): south = lax.ppermute(up, 'lat', [(i + 1, i) for i in range(lats - 1)])  2.86 us
    pallas_call x2, Pallas kernels, some_rows(): pl.pallas_call(kernel, out_shape=jax.ShapeDtypeStruct((blocks * CHUNK, PA...  2.51 us
    ppermute x1, starting transfers between devices, on_device(): south = lax.ppermute(up, 'lat', [(i + 1, i) for i in range(lats - 1)])  2.36 us
  transfers between devices with their start and end apart: 4, of which 3 were waited for; matrix products, arithmetic and copies ran while one was open for 0% of the time, Pallas kernels for 8%

profile of v6, /device:TPU:8, one launch (start us, length us, event | category | flops | bytes accessed | tf_op | source)
XLA Modules:
  0.0 32.1 jit_solution(15270029869964729521)
XLA Ops:
  0.6 0.0 copy-start
  0.6 3.4 %shard_map.122 = (f32[32,96,128]{2,1,0:T(8,128)S(1)}, f32[32,96,128]{2,1,0:T(8,128)S(1)}, bf16[512,192]{1,0:T(8,128)(2,1)S(1)}, f8e4m3fn[512,384]{1,0:T(32,128)(...) custom-call(f32[90,32,128]{2,1,0:T(8,128)} %t_hbm.1, ...), custom_call_target="tpu_custom_call" | custom-call | flops 1000000 | bytes 8000000 | tf_op jit(solution)/shard_map/pallas_call | solution.py:168
  4.0 3.5 %collective-permute-start = (f32[192,128]{1,0:T(8,128)S(1)}, f32[192,128]{1,0:T(8,128)S(1)}, u32[]{:S(2)}, u32[]{:S(2)}) collective-permute-start(f32[192,128]{1,0:T(8,128)S(1)} %get-tuple-element.26), channel_id=1, source_target_pairs={{0,1},{1,2},{2,3},{4,5},{5,6},{6,7},{8,9},{9,10},{10,11},{12,13},{... | collective-permute-start | bytes 294920 | tf_op jit(solution)/shard_map/ppermute | solution.py:543
  7.5 2.4 %collective-permute-start.1 = (f32[192,128]{1,0:T(8,128)S(1)}, f32[192,128]{1,0:T(8,128)S(1)}, u32[]{:S(2)}, u32[]{:S(2)}) collective-permute-start(f32[192,128]{1,0:T(8,128)S(1)} %get-tuple-element.27), channel_id=1, source_target_pairs={{1,0},{2,1},{3,2},{5,4},{6,5},{7,6},{9,8},{10,9},{11,10},{13,12},{... | collective-permute-start | bytes 294920 | tf_op jit(solution)/shard_map/ppermute | solution.py:544
  9.9 0.0 copy-done
  9.9 1.2 %shard_map.123.before.heat_a = f32[16,96,128]{2,1,0:T(8,128)S(1)} custom-call(s32[1,128]{1,0:T(1,128)S(1)} %concatenate.3.lit_row, f32[32,96,128]{2,1,0:T(8,128)S(1)} %get-tuple-element.17.t, f32[32,96,128]{2,1,0:T(8,128)S(1)} %get-tuple-element.18.m, bf16[512,192]{1,0:T(8,128)(2,1)S(1)} %get-tuple-element.19.w1s, ...), custom_call_target="tpu_custom_call" | custom-call | flops 5000000000 | bytes 8000000 | tf_op jit(solution)/shard_map/pallas_call | solution.py:363
  11.2 0.0 collective-permute-done.north_ref.north
  11.2 2.9 %collective-permute-done.1.south_ref.south = f32[192,128]{1,0:T(8,128)S(1)} collective-permute-done((f32[192,128]{1,0:T(8,128)S(1)}, f32[192,128]{1,0:T(8,128)S(1)}, u32[]{:S(2)}, u32[]{:S(2)}) %collective-permute-start.1) | collective-permute-done | bytes 98336 | tf_op jit(solution)/shard_map/ppermute | solution.py:544
  14.0 0.1 shard_map.125
  14.2 6.1 %collective-permute-start.3 = (f32[96,128]{1,0:T(8,128)S(1)}, f32[96,128]{1,0:T(8,128)S(1)}, u32[]{:S(2)}, u32[]{:S(2)}) collective-permute-start(f32[96,128]{1,0:T(8,128)S(1)} %get-tuple-element.30.mine_w), channel_id=1, source_target_pairs={{0,252},{4,0},{8,4},{12,8},{16,12},{20,16},{24,20},{28,24},{32,28}... | collective-permute-start | bytes 147464 | tf_op jit(solution)/shard_map/ppermute | solution.py:547
  20.3 0.0 collective-permute-start.2
  20.3 1.3 %shard_map.124.heat_b = f32[24,96,128]{2,1,0:T(8,128)S(1)} custom-call(s32[1,128]{1,0:T(1,128)S(1)} %concatenate.3.lit_row, f32[16,96,128]{2,1,0:T(8,128)S(1)} %shard_map.123.before.heat_a, f32[32,96,128]{2,1,0:T(8,128)S(1)} %get-tuple-element.17.t, f32[32,96,128]{2,1,0:T(8,128)S(1)} %get-tuple-element.18.m, bf16[512,192]{1,0:T(8,128)(2,1)S(1)} %get-tuple-element.19.w1s, ...), custom_call_target="tpu_custom_call" | custom-call | flops 5000000000 | bytes 8000000 | tf_op jit(solution)/shard_map/pallas_call | solution.py:363
  21.6 0.5 %collective-permute-done.3.east = f32[96,128]{1,0:T(8,128)S(1)} collective-permute-done((f32[96,128]{1,0:T(8,128)S(1)}, f32[96,128]{1,0:T(8,128)S(1)}, u32[]{:S(2)}, u32[]{:S(2)}) %collective-permute-start.3) | collective-permute-done | bytes 49184 | tf_op jit(solution)/shard_map/ppermute | solution.py:547
  22.0 5.1 %collective-permute-done.2.west = f32[96,128]{1,0:T(8,128)S(1)} collective-permute-done((f32[96,128]{1,0:T(8,128)S(1)}, f32[96,128]{1,0:T(8,128)S(1)}, u32[]{:S(2)}, u32[]{:S(2)}) %collective-permute-start.2) | collective-permute-done | bytes 49184 | tf_op jit(solution)/shard_map/ppermute | solution.py:548
  27.1 4.8 %shard_map.126 = (f32[90,32,128]{2,1,0:T(8,128)}, f32[90,32,128]{2,1,0:T(8,128)}) custom-call(s32[1,128]{1,0:T(1,128)S(1)} %concatenate.3.lit_row, f32[32,96,128]{2,1,0:T(8,128)S(1)} %get-tuple-element.17.t, f32[32,96,128]{2,1,0:T(8,128)S(1)} %get-tuple-element.18.m, bf16[512,192]{1,0:T(8,128)(2,1)S(1)} %get-tuple-element.19.w1s, ...), custom_call_target="tpu_custom_call" | custom-call | flops 10000000000 | bytes 8000000 | tf_op jit(solution)/shard_map/pallas_call | solution.py:520
  (1 shorter events, 0.0 us)
Async XLA Ops:
  0.6 9.3 %copy-start = (s32[32,1]{0,1:T(1,128)S(1)}, s32[32,1]{0,1:T(1,128)}, u32[]{:S(2)}) copy-start(s32[32,1]{0,1:T(1,128)} %param.14) | copy-start | bytes 388
  4.0 7.1 %collective-permute-start = (f32[192,128]{1,0:T(8,128)S(1)}, f32[192,128]{1,0:T(8,128)S(1)}, u32[]{:S(2)}, u32[]{:S(2)}) collective-permute-start(f32[192,128]{1,0:T(8,128)S(1)} %get-tuple-element.26), channel_id=1, source_target_pairs={{0,1},{1,2},{2,3},{4,5},{5,6},{6,7},{8,9},{9,10},{10,11},{12,13},{... | collective-permute-start | bytes 294920 | tf_op jit(solution)/shard_map/ppermute | solution.py:543
  7.5 6.5 %collective-permute-start.1 = (f32[192,128]{1,0:T(8,128)S(1)}, f32[192,128]{1,0:T(8,128)S(1)}, u32[]{:S(2)}, u32[]{:S(2)}) collective-permute-start(f32[192,128]{1,0:T(8,128)S(1)} %get-tuple-element.27), channel_id=1, source_target_pairs={{1,0},{2,1},{3,2},{5,4},{6,5},{7,6},{9,8},{10,9},{11,10},{13,12},{... | collective-permute-start | bytes 294920 | tf_op jit(solution)/shard_map/ppermute | solution.py:544
  14.2 7.9 %collective-permute-start.3 = (f32[96,128]{1,0:T(8,128)S(1)}, f32[96,128]{1,0:T(8,128)S(1)}, u32[]{:S(2)}, u32[]{:S(2)}) collective-permute-start(f32[96,128]{1,0:T(8,128)S(1)} %get-tuple-element.30.mine_w), channel_id=1, source_target_pairs={{0,252},{4,0},{8,4},{12,8},{16,12},{20,16},{24,20},{28,24},{32,28}... | collective-permute-start | bytes 147464 | tf_op jit(solution)/shard_map/ppermute | solution.py:547
  20.3 6.8 %collective-permute-start.2 = (f32[96,128]{1,0:T(8,128)S(1)}, f32[96,128]{1,0:T(8,128)S(1)}, u32[]{:S(2)}, u32[]{:S(2)}) collective-permute-start(f32[96,128]{1,0:T(8,128)S(1)} %get-tuple-element.31.mine_e), channel_id=1, source_target_pairs={{0,4},{4,8},{8,12},{12,16},{16,20},{20,24},{24,28},{28,32},{32,36}... | collective-permute-start | bytes 147464 | tf_op jit(solution)/shard_map/ppermute | solution.py:548

commit v7 on v6

--- a/solution.py
+++ b/solution.py
@@ -114,11 +114,17 @@
     state = [pltpu.make_async_copy(k_hbm, k, sems.at[1])] + rows(t_hbm, t, sems.at[1])
     inner = [pltpu.make_async_copy(w2_hbm.at[i], w2.at[i], sems.at[2 + i]) for i in range(2)]
     humid = [pltpu.make_async_copy(s_hbm, s, sems.at[4])] + rows(m_hbm, m, sems.at[4])
-    for copy in outer + state + inner + humid:
+    for copy in outer + inner + state + humid:
         copy.start()
     for copy in outer:
         copy.wait()
     bound = prepare_outer(w1, b1, b2, w4, b4, w1s, w18, w4s, bs, sc)
+    inner[0].wait()
+    prepare_inner(0, w2, w2s, w28)
+    bound = bound * jnp.max(jnp.sum(jnp.abs(w2[0]), axis=1, keepdims=True)) + jnp.max(jnp.abs(b2[...]))
+    put_scale(sc, 1, bound)
+    inner[1].wait()
+    prepare_inner(1, w2, w2s, w28)
     for copy in state:
         copy.wait()
     blank = jnp.zeros((PAD - LEV - 1, COLS), F32)
@@ -137,12 +143,6 @@
     up[PAD:] = t[1]
     down[0:PAD] = t[ROWS - 1]
     down[PAD:] = t[ROWS - 2]
-    inner[0].wait()
-    prepare_inner(0, w2, w2s, w28)
-    bound = bound * jnp.max(jnp.sum(jnp.abs(w2[0]), axis=1, keepdims=True)) + jnp.max(jnp.abs(b2[...]))
-    put_scale(sc, 1, bound)
-    inner[1].wait()
-    prepare_inner(1, w2, w2s, w28)
     for copy in humid:
         copy.wait()
     one = jnp.ones((1, COLS), F32)

time: 32.2 us -> 32.1 us (level)
  Pallas kernels: 10.8 us -> 21.8 us
  waiting for transfers between devices: 8.42 us -> 0.01 us
  starting transfers between devices: 12 us -> 9.25 us
    pallas_call x2, Pallas kernels: 2.51 us -> 14.7 us  [some_rows(): pl.pallas_call(kernel, out_shape=jax.ShapeDtypeStruct((blocks * CHUNK, PA...]
    ppermute x1, waiting for transfers between devices: 5.08 us -> 0.01 us  [on_device(): lax.ppermute(east, 'lon', [(i, (i + 1) % lons) for i in range(lons)])]
    ppermute x1, waiting for transfers between devices: 2.86 us -> 0.01 us  [on_device(): south = lax.ppermute(up, 'lat', [(i + 1, i) for i in range(lats - 1)])]
    ppermute x1, starting transfers between devices: 6.14 us -> 3.41 us  [on_device(): lax.ppermute(west, 'lon', [(i, (i - 1) % lons) for i in range(lons)])]
    pallas_call x1, Pallas kernels: 4.83 us -> 3.67 us  [last(): pl.pallas_call(last_kernel, out_shape=(whole, whole), in_specs=[VMEM] * 1...]
    ppermute x1, waiting for transfers between devices: 0.47 us -> 0.01 us  [on_device(): lax.ppermute(west, 'lon', [(i, (i - 1) % lons) for i in range(lons)])]
  transfers between devices with their start and end apart: 4 -> 4, of which waited for: 3 -> 0; matrix products, arithmetic and copies ran while one was open for 0% -> 0% of each run, Pallas kernels for 8% -> 46%
where the time goes in v7:
time: 32.1 us; the launch traced here: 32 us
  Pallas kernels  21.8 us (68%)
  starting transfers between devices  9.25 us (29%)
  between operations  0.9 us (3%)
    pallas_call x2, Pallas kernels, some_rows(): pl.pallas_call(kernel, out_shape=jax.ShapeDtypeStruct((blocks * CHUNK, PA...  14.7 us
    pallas_call x1, Pallas kernels, last(): pl.pallas_call(last_kernel, out_shape=(whole, whole), in_specs=[VMEM] * 1...  3.67 us
    ppermute x1, starting transfers between devices, on_device(): north = lax.ppermute(down, 'lat', [(i, i + 1) for i in range(lats - 1)])  3.48 us
    ppermute x1, starting transfers between devices, on_device(): lax.ppermute(west, 'lon', [(i, (i - 1) % lons) for i in range(lons)])  3.41 us
    pallas_call x1, Pallas kernels, load(): pl.pallas_call(load_kernel, out_shape=(TRACK, TRACK) + tuple((jax.ShapeDt...  3.28 us
    ppermute x1, starting transfers between devices, on_device(): south = lax.ppermute(up, 'lat', [(i + 1, i) for i in range(lats - 1)])  2.36 us
  transfers between devices with their start and end apart: 4, of which 0 were waited for; matrix products, arithmetic and copies ran while one was open for 0% of the time, Pallas kernels for 46%

profile of v7, /device:TPU:8, one launch (start us, length us, event | category | flops | bytes accessed | tf_op | source)
XLA Modules:
  0.0 32.0 jit_solution(14625051908402716617)
XLA Ops:
  0.6 0.0 copy-start
  0.6 3.3 %shard_map.122 = (f32[32,96,128]{2,1,0:T(8,128)S(1)}, f32[32,96,128]{2,1,0:T(8,128)S(1)}, bf16[512,192]{1,0:T(8,128)(2,1)S(1)}, f8e4m3fn[512,384]{1,0:T(32,128)(...) custom-call(f32[90,32,128]{2,1,0:T(8,128)} %t_hbm.1, ...), custom_call_target="tpu_custom_call" | custom-call | flops 1000000 | bytes 8000000 | tf_op jit(solution)/shard_map/pallas_call | solution.py:168
  3.9 3.5 %collective-permute-start = (f32[192,128]{1,0:T(8,128)S(1)}, f32[192,128]{1,0:T(8,128)S(1)}, u32[]{:S(2)}, u32[]{:S(2)}) collective-permute-start(f32[192,128]{1,0:T(8,128)S(1)} %get-tuple-element.26), channel_id=1, source_target_pairs={{0,1},{1,2},{2,3},{4,5},{5,6},{6,7},{8,9},{9,10},{10,11},{12,13},{... | collective-permute-start | bytes 294920 | tf_op jit(solution)/shard_map/ppermute | solution.py:543
  7.4 2.4 %collective-permute-start.1 = (f32[192,128]{1,0:T(8,128)S(1)}, f32[192,128]{1,0:T(8,128)S(1)}, u32[]{:S(2)}, u32[]{:S(2)}) collective-permute-start(f32[192,128]{1,0:T(8,128)S(1)} %get-tuple-element.27), channel_id=1, source_target_pairs={{1,0},{2,1},{3,2},{5,4},{6,5},{7,6},{9,8},{10,9},{11,10},{13,12},{... | collective-permute-start | bytes 294920 | tf_op jit(solution)/shard_map/ppermute | solution.py:544
  9.8 0.0 copy-done
  9.8 7.4 %shard_map.123.before.heat_a = f32[16,96,128]{2,1,0:T(8,128)S(1)} custom-call(s32[1,128]{1,0:T(1,128)S(1)} %concatenate.3.lit_row, f32[32,96,128]{2,1,0:T(8,128)S(1)} %get-tuple-element.17.t, f32[32,96,128]{2,1,0:T(8,128)S(1)} %get-tuple-element.18.m, bf16[512,192]{1,0:T(8,128)(2,1)S(1)} %get-tuple-element.19.w1s, ...), custom_call_target="tpu_custom_call" | custom-call | flops 5000000000 | bytes 8000000 | tf_op jit(solution)/shard_map/pallas_call | solution.py:363
  17.2 0.0 collective-permute-done.north_ref.north
  17.2 0.0 collective-permute-done.1.south_ref.south
  17.2 0.1 shard_map.125
  17.3 3.4 %collective-permute-start.3 = (f32[96,128]{1,0:T(8,128)S(1)}, f32[96,128]{1,0:T(8,128)S(1)}, u32[]{:S(2)}, u32[]{:S(2)}) collective-permute-start(f32[96,128]{1,0:T(8,128)S(1)} %get-tuple-element.30.mine_w), channel_id=1, source_target_pairs={{0,252},{4,0},{8,4},{12,8},{16,12},{20,16},{24,20},{28,24},{32,28}... | collective-permute-start | bytes 147464 | tf_op jit(solution)/shard_map/ppermute | solution.py:547
  20.7 0.0 collective-permute-start.2
  20.7 7.4 %shard_map.124.heat_b = f32[24,96,128]{2,1,0:T(8,128)S(1)} custom-call(s32[1,128]{1,0:T(1,128)S(1)} %concatenate.3.lit_row, f32[16,96,128]{2,1,0:T(8,128)S(1)} %shard_map.123.before.heat_a, f32[32,96,128]{2,1,0:T(8,128)S(1)} %get-tuple-element.17.t, f32[32,96,128]{2,1,0:T(8,128)S(1)} %get-tuple-element.18.m, bf16[512,192]{1,0:T(8,128)(2,1)S(1)} %get-tuple-element.19.w1s, ...), custom_call_target="tpu_custom_call" | custom-call | flops 5000000000 | bytes 8000000 | tf_op jit(solution)/shard_map/pallas_call | solution.py:363
  28.1 0.0 collective-permute-done.3.east
  28.1 0.0 collective-permute-done.2.west
  28.1 3.7 %shard_map.126 = (f32[90,32,128]{2,1,0:T(8,128)}, f32[90,32,128]{2,1,0:T(8,128)}) custom-call(s32[1,128]{1,0:T(1,128)S(1)} %concatenate.3.lit_row, f32[32,96,128]{2,1,0:T(8,128)S(1)} %get-tuple-element.17.t, f32[32,96,128]{2,1,0:T(8,128)S(1)} %get-tuple-element.18.m, bf16[512,192]{1,0:T(8,128)(2,1)S(1)} %get-tuple-element.19.w1s, ...), custom_call_target="tpu_custom_call" | custom-call | flops 10000000000 | bytes 8000000 | tf_op jit(solution)/shard_map/pallas_call | solution.py:520
  (1 shorter events, 0.0 us)
Async XLA Ops:
  0.6 9.2 %copy-start = (s32[32,1]{0,1:T(1,128)S(1)}, s32[32,1]{0,1:T(1,128)}, u32[]{:S(2)}) copy-start(s32[32,1]{0,1:T(1,128)} %param.14) | copy-start | bytes 388
  3.9 13.3 %collective-permute-start = (f32[192,128]{1,0:T(8,128)S(1)}, f32[192,128]{1,0:T(8,128)S(1)}, u32[]{:S(2)}, u32[]{:S(2)}) collective-permute-start(f32[192,128]{1,0:T(8,128)S(1)} %get-tuple-element.26), channel_id=1, source_target_pairs={{0,1},{1,2},{2,3},{4,5},{5,6},{6,7},{8,9},{9,10},{10,11},{12,13},{... | collective-permute-start | bytes 294920 | tf_op jit(solution)/shard_map/ppermute | solution.py:543
  7.4 9.8 %collective-permute-start.1 = (f32[192,128]{1,0:T(8,128)S(1)}, f32[192,128]{1,0:T(8,128)S(1)}, u32[]{:S(2)}, u32[]{:S(2)}) collective-permute-start(f32[192,128]{1,0:T(8,128)S(1)} %get-tuple-element.27), channel_id=1, source_target_pairs={{1,0},{2,1},{3,2},{5,4},{6,5},{7,6},{9,8},{10,9},{11,10},{13,12},{... | collective-permute-start | bytes 294920 | tf_op jit(solution)/shard_map/ppermute | solution.py:544
  17.3 10.8 %collective-permute-start.3 = (f32[96,128]{1,0:T(8,128)S(1)}, f32[96,128]{1,0:T(8,128)S(1)}, u32[]{:S(2)}, u32[]{:S(2)}) collective-permute-start(f32[96,128]{1,0:T(8,128)S(1)} %get-tuple-element.30.mine_w), channel_id=1, source_target_pairs={{0,252},{4,0},{8,4},{12,8},{16,12},{20,16},{24,20},{28,24},{32,28}... | collective-permute-start | bytes 147464 | tf_op jit(solution)/shard_map/ppermute | solution.py:547
  20.7 7.4 %collective-permute-start.2 = (f32[96,128]{1,0:T(8,128)S(1)}, f32[96,128]{1,0:T(8,128)S(1)}, u32[]{:S(2)}, u32[]{:S(2)}) collective-permute-start(f32[96,128]{1,0:T(8,128)S(1)} %get-tuple-element.31.mine_e), channel_id=1, source_target_pairs={{0,4},{4,8},{8,12},{12,16},{16,20},{20,24},{24,28},{28,32},{32,36}... | collective-permute-start | bytes 147464 | tf_op jit(solution)/shard_map/ppermute | solution.py:548
